TPU v7x, 256 devices: a whole 4x4x8 slice. The times are simulated.
256 devices in a mesh: dp: 16 (over y, z_lo), tensor: 16 (over x, z_hi, core).
Axes of the slice: x: 4, y: 4, z: 8 (z_hi: 2, z_lo: 4; z = z_hi * 4 + z_lo), core: 2. Of those that a mesh axis runs over, the one named last changes fastest.
Arguments:
- activations: bfloat16 [8192, 4096], P(('dp', 'tensor')), may hold values from -24 to 24
- token_scales: float32 [8192], P(('dp', 'tensor')), may hold values from 0.3 to 3
- out_grad: bfloat16 [8192, 14336], P('dp', 'tensor'), may hold values from -6 to 6
- weight: bfloat16 [4096, 14336], P('dp', 'tensor'), may hold values from -0.09375 to 0.09375
- logits: float32 [6, 1024, 14336], P(None, 'dp', 'tensor'), may hold values from -8 to 8
- gumbel: float32 [6, 1024, 14336], P(None, 'dp', 'tensor'), may hold values from -2.7 to 13.9, as said below
Outputs:
- input_grad: bfloat16 [8192, 4096], P(('dp', 'tensor'))
- logit_grad: float32 [6, 1024, 14336], P(None, 'dp', 'tensor')
Inputs may be any that keep to these rules, and one draw needn't show every extreme that they name: `gumbel`: entries are independent.
All inputs are finite; a program needn't handle non-finite values.
Results may differ from a plain program's by a relative error of at most 0.0049.
Values may be sent and summed in bfloat16 or wider, within the bound.
No kernel may reach another device: no remote copies, remote signals or barrier semaphores. Data moves between devices by JAX's collectives and lax.ppermute only.
A program may use at most 128 MiB of HBM per device.

v0:
```python
import jax
import jax.numpy as jnp
from jax import lax
from jax.sharding import Mesh, PartitionSpec as P

PATTERN_PAIRS = ((0, 1), (0, 2), (0, 3), (1, 2), (1, 3), (2, 3))
inverse_temp = 0.5
F32, BF16 = jnp.float32, jnp.bfloat16


def soft_mask(logits, gumbel):
    exponent = jnp.exp((logits + gumbel) * inverse_temp)
    chances = exponent / jnp.sum(exponent, axis=0)
    kept_slots = []
    for position in range(4):
        chosen = [chances[which] for which in range(6) if position in PATTERN_PAIRS[which]]
        kept_slots.append(chosen[0] + chosen[1] + chosen[2])
    mask_full = jnp.stack(kept_slots, axis=1)
    return (chances, mask_full.reshape(-1, mask_full.shape[2]))


def logit_grads(chances, mask_grad):
    groups = mask_grad.reshape(-1, 4, mask_grad.shape[1])
    pattern = jnp.stack(
        [
            groups[:, first_slot] + groups[:, second_slot]
            for first_slot, second_slot in PATTERN_PAIRS
        ],
        axis=0,
    )
    average = jnp.sum(chances * pattern, axis=0)
    return chances * (pattern - average) * inverse_temp


def shift(value, axis, by):
    size = lax.axis_size(axis)
    return lax.ppermute(value, axis, [(i, (i + by) % size) for i in range(size)])


def tie(*values):
    return lax.optimization_barrier(values)


def in_place(parts, which):
    which = which.reshape((-1,) + (1,) * parts[0].ndim)
    placed = parts[0][None]
    for k in range(1, len(parts)):
        placed = jnp.where(which == k, parts[k][None], placed)
    return placed


def body(activations, token_scales, out_grad, weight, logits, gumbel):
    y, zl, x = lax.axis_index("y"), lax.axis_index("zl"), lax.axis_index("x")
    zh, core = lax.axis_index("zh"), lax.axis_index("c")
    rows, features = activations.shape
    depth, hidden = weight.shape
    wide = 4 * depth

    own = out_grad.reshape(8, 2, rows, hidden).transpose(1, 0, 2, 3).reshape(16 * rows, hidden)
    half = 8 * rows

    local = (activations.astype(F32) * token_scales[:, None]).astype(BF16)
    pieces = []
    for k in range(4):
        pieces.append(
            jnp.concatenate(
                [
                    lax.dynamic_slice_in_dim(
                        local, ((y + k) % 4) * wide + ((zl + m) % 4) * depth, depth, 1
                    )
                    for m in range(4)
                ],
                axis=1,
            )
        )
    scaled = jnp.stack([pieces[0]] + [shift(pieces[k], "y", k) for k in (1, 2, 3)], axis=0)
    scaled, own = tie(scaled, own)

    chances, mask_full = soft_mask(logits, gumbel)
    weight_wide = weight.astype(F32)
    masked = (weight_wide * mask_full).astype(BF16)

    other = shift(scaled, "zh", 1)
    masked_1 = shift(masked, "zl", -1)
    below, above = shift(own, "y", 1), shift(own, "y", -1)
    other, masked_1, below, above = tie(other, masked_1, below, above)
    scaled = in_place([scaled, other], jnp.where(zh == 0, jnp.arange(2), 1 - jnp.arange(2)))

    masked_2 = shift(masked_1, "zl", -1)
    far_a, far_b = shift(below[:half], "y", 1), shift(above[half:], "y", -1)
    scaled_1, scaled_3 = shift(scaled, "x", 1), shift(scaled, "x", 3)
    masked_2, far_a, far_b, scaled, scaled_1, scaled_3 = tie(
        masked_2, far_a, far_b, scaled, scaled_1, scaled_3
    )
    grads = jnp.concatenate([own, below, far_a, far_b, above], axis=0)

    masked_3 = shift(masked_2, "zl", -1)
    scaled_2 = shift(scaled, "x", 2)
    near = (scaled, scaled_1, scaled_3)
    near_core = shift(jnp.stack(near, axis=0), "c", 1)
    scaled_2, near_core = tie(scaled_2, near_core)
    far_core = shift(scaled_2, "c", 1)
    rows_of = jnp.zeros((4, 2, 4, 2, rows, wide), BF16)
    for part, j, on_core in (
        (near[0], 0, core),
        (near[1], 1, core),
        (near[2], 3, core),
        (near_core[0], 0, 1 - core),
        (near_core[1], 1, 1 - core),
        (near_core[2], 3, 1 - core),
        (scaled_2, 2, core),
        (far_core, 2, 1 - core),
    ):
        part = part.transpose(1, 0, 2, 3)[:, None, None]
        rows_of = lax.dynamic_update_slice(rows_of, part, (0, on_core, (x - j) % 4, 0, 0, 0))
    scaled = rows_of.reshape(4 * 16 * rows, wide)

    grad_w = [
        lax.dot_general(
            scaled[:, m * depth : (m + 1) * depth],
            grads,
            (((0,), (0,)), ((), ())),
            preferred_element_type=F32,
        )
        for m in range(4)
    ]
    moving = grad_w[1].astype(BF16)

    grads = grads.reshape(4, 2, half, hidden)
    mine = lax.dynamic_index_in_dim(grads, core, 1, False).reshape(4 * half, hidden)
    its = lax.dynamic_index_in_dim(grads, 1 - core, 1, False).reshape(4 * half, hidden)
    sent, totals = [], []
    for pair in ((masked, masked_1), (masked_2, masked_3)):
        pair = jnp.concatenate(pair, axis=0)
        given = lax.dot_general(
            its, pair, (((1,), (1,)), ((), ())), preferred_element_type=F32
        ).astype(BF16)
        given = shift(given, "c", 1)
        kept = lax.dot_general(
            mine, pair, (((1,), (1,)), ((), ())), preferred_element_type=F32
        )
        total = (kept + given.astype(F32)).reshape(4, 4, 2 * rows, 2 * depth)
        totals.append(lax.dynamic_index_in_dim(total, x, 1, False))
        total = total.astype(BF16)
        sent.append([lax.dynamic_index_in_dim(total, (x - j) % 4, 1, False) for j in (1, 2, 3)])

    moving = (shift(moving, "zl", -1).astype(F32) + grad_w[2]).astype(BF16)

    first = [shift(sent[0][j - 1], "x", -j) for j in (1, 2, 3)]
    out = tie(*first, *sent[1])
    first, second = out[:3], out[3:]
    second = [shift(second[j - 1], "x", -j) for j in (1, 2, 3)]
    moving = shift(moving, "zl", -1)
    moving, *second = tie(moving, *second)
    moving = (moving.astype(F32) + grad_w[3]).astype(BF16)

    moving = shift(moving, "zl", -1)

    total = jnp.concatenate(
        [
            base + parts[0].astype(F32) + parts[1].astype(F32) + parts[2].astype(F32)
            for base, parts in zip(totals, (first, second))
        ],
        axis=-1,
    ).reshape(4, 2, rows, wide)
    other = shift(lax.dynamic_index_in_dim(total, 1 - zh, 1, False).astype(BF16), "zh", 1)

    total = lax.dynamic_index_in_dim(total, zh, 1, False) + other.astype(F32)
    total = total.astype(BF16)
    total = jnp.concatenate([total, total], axis=2)
    total = lax.dynamic_slice_in_dim(total, ((4 - zl) % 4) * depth, wide, 2)
    parts = [total[0]] + [shift(total[k], "y", -k) for k in (1, 2, 3)]
    input_grad = jnp.zeros((rows, features), BF16)
    for k in range(4):
        input_grad = lax.dynamic_update_slice(input_grad, parts[k], (0, ((y + k) % 4) * wide))

    return (input_grad, logit_grads(chances, (moving.astype(F32) + grad_w[0]) * weight_wide))


def solution(mesh):
    fine = Mesh(mesh.devices.reshape(4, 4, 4, 2, 2), ("y", "zl", "x", "zh", "c"))
    dp, tensor = ("y", "zl"), ("x", "zh", "c")
    return jax.shard_map(
        body,
        mesh=fine,
        in_specs=(
            P(dp + tensor, None),
            P(dp + tensor),
            P(dp, tensor),
            P(dp, tensor),
            P(None, dp, tensor),
            P(None, dp, tensor),
        ),
        out_specs=(P(dp + tensor, None), P(None, dp, tensor)),
        check_vma=False,
    )
```

profile of v0, /device:TPU:1, one launch (start us, length us, event | category | flops | bytes accessed | tf_op | source)
XLA Modules:
  0.0 153.7 jit_solution(9093431198486174444)
XLA Ops:
  2.2 3.6 %collective-permute-start.2 = (bf16[32,1024]{1,0:T(8,128)(2,1)S(1)}, bf16[32,1024]{1,0:T(8,128)(2,1)S(1)}, u32[]{:S(2)}, u32[]{:S(2)}) collective-permute-start(bf16[32,1024]{1,0:T(8,128)(2,1)S(1)} %pad_maximum_fusion.11), channel_id=1, source_target_pairs={{0,192},{64,0},{128,64},{192,128},{1,193},{65,1},{129,65},{193,129... | collective-permute-start | bytes 196616 | tf_op jit(solution)/shard_map/ppermute | solution.py:37
  6.9 2.2 %copy.25 = bf16[2,8,32,896]{3,2,1,0:T(8,128)(2,1)} copy(bf16[2,8,32,896]{3,2,0,1:T(8,128)(2,1)} %bitcast.159) | data formatting | bytes 1835008 | tf_op jit(solution)/shard_map/transpose | solution.py:59
  12.5 1.5 collective-permute-start.6
  16.2 4.4 %collective-permute-start.4 = (bf16[256,896]{1,0:T(8,128)(2,1)S(1)}, bf16[256,896]{1,0:T(8,128)(2,1)S(1)}, u32[]{:S(2)}, u32[]{:S(2)}) collective-permute-start(bf16[256,896]{1,0:T(8,128)(2,1)S(1)} %fusion.7), channel_id=1, source_target_pairs={{0,48},{16,0},{32,16},{48,32},{1,49},{17,1},{33,17},{49,33},{2,50}... | collective-permute-start | bytes 1376264 | tf_op jit(solution)/shard_map/ppermute | solution.py:37
  20.6 4.2 %collective-permute-start.3 = (bf16[4,32,1024]{2,1,0:T(8,128)(2,1)S(1)}, bf16[4,32,1024]{2,1,0:T(8,128)(2,1)S(1)}, u32[]{:S(2)}, u32[]{:S(2)}) collective-permute-start(bf16[4,32,1024]{2,1,0:T(8,128)(2,1)S(1)} %pad_maximum_fusion.8), channel_id=1, source_target_pairs={{0,2},{2,0},{1,3},{3,1},{4,6},{6,4},{5,7},{7,5},{8,10},{10,8},{9,1... | collective-permute-start | bytes 786440 | tf_op jit(solution)/shard_map/ppermute | solution.py:37
  24.8 18.9 %collective-permute-done.3 = bf16[4,32,1024]{2,1,0:T(8,128)(2,1)S(1)} collective-permute-done((bf16[4,32,1024]{2,1,0:T(8,128)(2,1)S(1)}, bf16[4,32,1024]{2,1,0:T(8,128)(2,1)S(1)}, u32[]{:S(2)}, u32[]{:S(2)}) %collective-permute-start.3) | collective-permute-done | bytes 262176 | tf_op jit(solution)/shard_map/ppermute | solution.py:37
  45.9 1.5 collective-permute-start.11
  47.9 1.8 %slice.89 = bf16[256,896]{1,0:T(8,128)(2,1)} slice(bf16[512,896]{1,0:T(8,128)(2,1)} %collective-permute-done.5), slice={[0:256], [0:896]} | slice | bytes 917504 | tf_op jit(solution)/shard_map/slice | solution.py:90
  50.7 1.8 %slice.90 = bf16[256,896]{1,0:T(8,128)(2,1)} slice(bf16[512,896]{1,0:T(8,128)(2,1)} %collective-permute-done.6), slice={[256:512], [0:896]} | slice | bytes 917504 | tf_op jit(solution)/shard_map/slice | solution.py:90
  52.5 1.7 %collective-permute-start.9 = (bf16[256,896]{1,0:T(8,128)(2,1)}, bf16[256,896]{1,0:T(8,128)(2,1)}, u32[]{:S(2)}, u32[]{:S(2)}) collective-permute-start(bf16[256,896]{1,0:T(8,128)(2,1)} %slice.90), channel_id=1, source_target_pairs={{0,192},{64,0},{128,64},{192,128},{1,193},{65,1},{129,65},{193,129... | collective-permute-start | bytes 1376264 | tf_op jit(solution)/shard_map/ppermute | solution.py:37
  55.5 1.3 constant_dynamic-update-slice_fusion.3
  56.8 2.0 %collective-permute-done.8 = bf16[256,896]{1,0:T(8,128)(2,1)} collective-permute-done((bf16[256,896]{1,0:T(8,128)(2,1)}, bf16[256,896]{1,0:T(8,128)(2,1)}, u32[]{:S(2)}, u32[]{:S(2)}) %collective-permute-start.8) | collective-permute-done | bytes 458784 | tf_op jit(solution)/shard_map/ppermute | solution.py:37
  58.8 1.9 %collective-permute-done.9 = bf16[256,896]{1,0:T(8,128)(2,1)} collective-permute-done((bf16[256,896]{1,0:T(8,128)(2,1)}, bf16[256,896]{1,0:T(8,128)(2,1)}, u32[]{:S(2)}, u32[]{:S(2)}) %collective-permute-start.9) | collective-permute-done | bytes 458784 | tf_op jit(solution)/shard_map/ppermute | solution.py:37
  64.5 1.5 collective-permute-start.18
  66.2 5.9 %collective-permute-start.19 = (bf16[3,2,4,32,1024]{4,3,1,2,0:T(8,128)(2,1)S(1)}, bf16[3,2,4,32,1024]{4,3,1,2,0:T(8,128)(2,1)S(1)}, u32[]{:S(2)}, u32[]{:S(2)}) collective-permute-start(bf16[3,2,4,32,1024]{4,3,1,2,0:T(8,128)(2,1)S(1)} %pad_maximum_fusion), channel_id=1, source_target_pairs={{0,1},{1,0},{2,3},{3,2},{4,5},{5,4},{6,7},{7,6},{8,9},{9,8},{10,11... | collective-permute-start | bytes 4718600 | tf_op jit(solution)/shard_map/ppermute | solution.py:37
  77.2 3.2 %collective-permute-start.20 = (bf16[2,4,32,1024]{3,2,0,1:T(8,128)(2,1)S(1)}, bf16[2,4,32,1024]{3,2,0,1:T(8,128)(2,1)S(1)}, u32[]{:S(2)}, u32[]{:S(2)}) collective-permute-start(bf16[2,4,32,1024]{3,2,0,1:T(8,128)(2,1)S(1)} %collective-permute-done.18), channel_id=1, source_target_pairs={{0,1},{1,0},{2,3},{3,2},{4,5},{5,4},{6,7},{7,6},{8,9},{9,8},{10,11... | collective-permute-start | bytes 1572872 | tf_op jit(solution)/shard_map/ppermute | solution.py:37
  84.9 1.6 %collective-permute-start.13 = (bf16[4,64,512]{2,1,0:T(8,128)(2,1)S(1)}, bf16[4,64,512]{2,1,0:T(8,128)(2,1)S(1)}, u32[]{:S(2)}, u32[]{:S(2)}) collective-permute-start(bf16[4,64,512]{2,1,0:T(8,128)(2,1)S(1)} %get-tuple-element.61), channel_id=1, source_target_pairs={{0,12},{4,0},{8,4},{12,8},{1,13},{5,1},{9,5},{13,9},{2,14},{6,2},{... | collective-permute-start | bytes 786440 | tf_op jit(solution)/shard_map/ppermute | solution.py:37
  87.6 7.8 %collective-permute-done.21 = bf16[256,896]{1,0:T(8,128)(2,1)S(1)} collective-permute-done((bf16[256,896]{1,0:T(8,128)(2,1)S(1)}, bf16[256,896]{1,0:T(8,128)(2,1)S(1)}, u32[]{:S(2)}, u32[]{:S(2)}) %collective-permute-start.21) | collective-permute-done | bytes 458784 | tf_op jit(solution)/shard_map/ppermute | solution.py:37
  95.5 2.1 %add_convert_fusion.1 = bf16[256,896]{1,0:T(8,128)(2,1)} fusion(bf16[256,896]{1,0:T(8,128)(2,1)S(1)} %collective-permute-done.21, bf16[2048,896]{1,0:T(8,128)(2,1)S(1)} %constant_dynamic-update-slice_fusion, bf16[2048,1024]{1,0:T(8,128)(2,1)S(1)} %bitcast.144), kind=kOutput, calls=%fused_computation.23 | convolution fusion | flops 940212224 | bytes 5636096 | tf_op jit(solution)/shard_map/dot_general | solution.py:119
  97.5 1.5 collective-permute-start.22
  103.3 1.8 %collective-permute-start.23 = (bf16[4,64,512]{2,1,0:T(8,128)(2,1)}, bf16[4,64,512]{2,1,0:T(8,128)(2,1)}, u32[]{:S(2)}, u32[]{:S(2)}) collective-permute-start(bf16[4,64,512]{2,1,0:T(8,128)(2,1)} %get-tuple-element.43), channel_id=1, source_target_pairs={{0,12},{4,0},{8,4},{12,8},{1,13},{5,1},{9,5},{13,9},{2,14},{6,2},{... | collective-permute-start | bytes 786440 | tf_op jit(solution)/shard_map/ppermute | solution.py:37
  107.5 2.8 %collective-permute-done.23 = bf16[4,64,512]{2,1,0:T(8,128)(2,1)} collective-permute-done((bf16[4,64,512]{2,1,0:T(8,128)(2,1)}, bf16[4,64,512]{2,1,0:T(8,128)(2,1)}, u32[]{:S(2)}, u32[]{:S(2)}) %collective-permute-start.23) | collective-permute-done | bytes 262176 | tf_op jit(solution)/shard_map/ppermute | solution.py:37
  110.3 3.0 %collective-permute-done.24 = bf16[4,64,512]{2,1,0:T(8,128)(2,1)} collective-permute-done((bf16[4,64,512]{2,1,0:T(8,128)(2,1)}, bf16[4,64,512]{2,1,0:T(8,128)(2,1)}, u32[]{:S(2)}, u32[]{:S(2)}) %collective-permute-start.24) | collective-permute-done | bytes 262176 | tf_op jit(solution)/shard_map/ppermute | solution.py:37
  113.3 7.4 %collective-permute-done.25 = bf16[4,64,512]{2,1,0:T(8,128)(2,1)} collective-permute-done((bf16[4,64,512]{2,1,0:T(8,128)(2,1)}, bf16[4,64,512]{2,1,0:T(8,128)(2,1)}, u32[]{:S(2)}, u32[]{:S(2)}) %collective-permute-start.25) | collective-permute-done | bytes 262176 | tf_op jit(solution)/shard_map/ppermute | solution.py:37
  120.8 1.4 fusion.11
  122.3 1.4 collective-permute-start.26
  123.7 2.6 %add_convert_fusion = bf16[256,896]{1,0:T(8,128)(2,1)S(1)} fusion(bf16[256,896]{1,0:T(8,128)(2,1)} %collective-permute-done.22, bf16[2048,896]{1,0:T(8,128)(2,1)S(1)} %copy-done.1, bf16[2048,1024]{1,0:T(8,128)(2,1)} %bitcast.145), kind=kOutput, calls=%fused_computation.22 | convolution fusion | flops 940212224 | bytes 5636096 | tf_op jit(solution)/shard_map/dot_general | solution.py:119
  126.4 1.5 collective-permute-start.30
  127.9 11.8 %collective-permute-done.26 = bf16[4,32,1024]{2,1,0:T(8,128)(2,1)S(1)} collective-permute-done((bf16[4,32,1024]{2,1,0:T(8,128)(2,1)S(1)}, bf16[4,32,1024]{2,1,0:T(8,128)(2,1)S(1)}, u32[]{:S(2)}, u32[]{:S(2)}) %collective-permute-start.26) | collective-permute-done | bytes 262176 | tf_op jit(solution)/shard_map/ppermute | solution.py:37
  139.9 3.5 %collective-permute-start.27 = (bf16[32,1024]{1,0:T(8,128)(2,1)S(1)}, bf16[32,1024]{1,0:T(8,128)(2,1)S(1)}, u32[]{:S(2)}, u32[]{:S(2)}) collective-permute-start(bf16[32,1024]{1,0:T(8,128)(2,1)S(1)} %get-tuple-element.68), channel_id=1, source_target_pairs={{0,192},{64,0},{128,64},{192,128},{1,193},{65,1},{129,65},{193,129... | collective-permute-start | bytes 196616 | tf_op jit(solution)/shard_map/ppermute | solution.py:37
  144.8 3.4 %collective-permute-done.28 = bf16[32,1024]{1,0:T(8,128)(2,1)S(1)} collective-permute-done((bf16[32,1024]{1,0:T(8,128)(2,1)S(1)}, bf16[32,1024]{1,0:T(8,128)(2,1)S(1)}, u32[]{:S(2)}, u32[]{:S(2)}) %collective-permute-start.28) | collective-permute-done | bytes 65568 | tf_op jit(solution)/shard_map/ppermute | solution.py:37
  148.5 2.6 %convert_multiply_fusion = f32[256,896]{1,0:T(8,128)S(1)} fusion(bf16[256,896]{1,0:T(8,128)(2,1)S(1)} %copy-done.7, bf16[256,896]{1,0:T(8,128)(2,1)S(1)} %collective-permute-done.30, bf16[2048,896]{1,0:T(8,128)(2,1)S(1)} %copy-done.1, bf16[2048,1024]{1,0:T(8,128)(2,1)} %bitcast.146), kind=kOutput, calls=%fused_computation.9 | convolution fusion | flops 940441600 | bytes 6553600 | tf_op jit(solution)/shard_map/dot_general | solution.py:119
  (132 shorter events, 38.6 us)
Async XLA Ops:
  2.2 8.5 %collective-permute-start.2 = (bf16[32,1024]{1,0:T(8,128)(2,1)S(1)}, bf16[32,1024]{1,0:T(8,128)(2,1)S(1)}, u32[]{:S(2)}, u32[]{:S(2)}) collective-permute-start(bf16[32,1024]{1,0:T(8,128)(2,1)S(1)} %pad_maximum_fusion.11), channel_id=1, source_target_pairs={{0,192},{64,0},{128,64},{192,128},{1,193},{65,1},{129,65},{193,129... | collective-permute-start | bytes 196616 | tf_op jit(solution)/shard_map/ppermute | solution.py:37
  5.9 4.9 %collective-permute-start.1 = (bf16[32,1024]{1,0:T(8,128)(2,1)S(1)}, bf16[32,1024]{1,0:T(8,128)(2,1)S(1)}, u32[]{:S(2)}, u32[]{:S(2)}) collective-permute-start(bf16[32,1024]{1,0:T(8,128)(2,1)S(1)} %pad_maximum_fusion.10), channel_id=1, source_target_pairs={{0,128},{64,192},{128,0},{192,64},{1,129},{65,193},{129,1},{193,65... | collective-permute-start | bytes 196616 | tf_op jit(solution)/shard_map/ppermute | solution.py:37
  6.2 5.0 %collective-permute-start = (bf16[32,1024]{1,0:T(8,128)(2,1)S(1)}, bf16[32,1024]{1,0:T(8,128)(2,1)S(1)}, u32[]{:S(2)}, u32[]{:S(2)}) collective-permute-start(bf16[32,1024]{1,0:T(8,128)(2,1)S(1)} %pad_maximum_fusion.9), channel_id=1, source_target_pairs={{0,64},{64,128},{128,192},{192,0},{1,65},{65,129},{129,193},{193,1... | collective-permute-start | bytes 196616 | tf_op jit(solution)/shard_map/ppermute | solution.py:37
  11.2 32.5 %collective-permute-start.5 = (bf16[512,896]{1,0:T(8,128)(2,1)}, bf16[512,896]{1,0:T(8,128)(2,1)}, u32[]{:S(2)}, u32[]{:S(2)}) collective-permute-start(bf16[512,896]{1,0:T(8,128)(2,1)} %bitcast.6), channel_id=1, source_target_pairs={{0,64},{64,128},{128,192},{192,0},{1,65},{65,129},{129,193},{193,1... | collective-permute-start | bytes 2752520 | tf_op jit(solution)/shard_map/ppermute | solution.py:37
  12.5 31.2 %collective-permute-start.6 = (bf16[512,896]{1,0:T(8,128)(2,1)}, bf16[512,896]{1,0:T(8,128)(2,1)}, u32[]{:S(2)}, u32[]{:S(2)}) collective-permute-start(bf16[512,896]{1,0:T(8,128)(2,1)} %bitcast.6), channel_id=1, source_target_pairs={{0,192},{64,0},{128,64},{192,128},{1,193},{65,1},{129,65},{193,129... | collective-permute-start | bytes 2752520 | tf_op jit(solution)/shard_map/ppermute | solution.py:37
  16.2 27.5 %collective-permute-start.4 = (bf16[256,896]{1,0:T(8,128)(2,1)S(1)}, bf16[256,896]{1,0:T(8,128)(2,1)S(1)}, u32[]{:S(2)}, u32[]{:S(2)}) collective-permute-start(bf16[256,896]{1,0:T(8,128)(2,1)S(1)} %fusion.7), channel_id=1, source_target_pairs={{0,48},{16,0},{32,16},{48,32},{1,49},{17,1},{33,17},{49,33},{2,50}... | collective-permute-start | bytes 1376264 | tf_op jit(solution)/shard_map/ppermute | solution.py:37
  20.6 23.1 %collective-permute-start.3 = (bf16[4,32,1024]{2,1,0:T(8,128)(2,1)S(1)}, bf16[4,32,1024]{2,1,0:T(8,128)(2,1)S(1)}, u32[]{:S(2)}, u32[]{:S(2)}) collective-permute-start(bf16[4,32,1024]{2,1,0:T(8,128)(2,1)S(1)} %pad_maximum_fusion.8), channel_id=1, source_target_pairs={{0,2},{2,0},{1,3},{3,1},{4,6},{6,4},{5,7},{7,5},{8,10},{10,8},{9,1... | collective-permute-start | bytes 786440 | tf_op jit(solution)/shard_map/ppermute | solution.py:37
  44.6 16.1 %collective-permute-start.10 = (bf16[2,4,32,1024]{3,2,0,1:T(8,128)(2,1)S(1)}, bf16[2,4,32,1024]{3,2,0,1:T(8,128)(2,1)S(1)}, u32[]{:S(2)}, u32[]{:S(2)}) collective-permute-start(bf16[2,4,32,1024]{3,2,0,1:T(8,128)(2,1)S(1)} %broadcast_select_fusion), channel_id=1, source_target_pairs={{0,4},{4,8},{8,12},{12,0},{1,5},{5,9},{9,13},{13,1},{2,6},{6,10},{... | collective-permute-start | bytes 1572872 | tf_op jit(solution)/shard_map/ppermute | solution.py:37
  45.9 14.8 %collective-permute-start.11 = (bf16[2,4,32,1024]{3,2,0,1:T(8,128)(2,1)S(1)}, bf16[2,4,32,1024]{3,2,0,1:T(8,128)(2,1)S(1)}, u32[]{:S(2)}, u32[]{:S(2)}) collective-permute-start(bf16[2,4,32,1024]{3,2,0,1:T(8,128)(2,1)S(1)} %broadcast_select_fusion), channel_id=1, source_target_pairs={{0,12},{4,0},{8,4},{12,8},{1,13},{5,1},{9,5},{13,9},{2,14},{6,2},{... | collective-permute-start | bytes 1572872 | tf_op jit(solution)/shard_map/ppermute | solution.py:37
  47.4 9.4 %collective-permute-start.7 = (bf16[256,896]{1,0:T(8,128)(2,1)}, bf16[256,896]{1,0:T(8,128)(2,1)S(1)}, u32[]{:S(2)}, u32[]{:S(2)}) collective-permute-start(bf16[256,896]{1,0:T(8,128)(2,1)} %copy-done.14), channel_id=1, source_target_pairs={{0,48},{16,0},{32,16},{48,32},{1,49},{17,1},{33,17},{49,33},{2,50}... | collective-permute-start | bytes 1376264 | tf_op jit(solution)/shard_map/ppermute | solution.py:37
  49.7 9.0 %collective-permute-start.8 = (bf16[256,896]{1,0:T(8,128)(2,1)}, bf16[256,896]{1,0:T(8,128)(2,1)}, u32[]{:S(2)}, u32[]{:S(2)}) collective-permute-start(bf16[256,896]{1,0:T(8,128)(2,1)} %slice.89), channel_id=1, source_target_pairs={{0,64},{64,128},{128,192},{192,0},{1,65},{65,129},{129,193},{193,1... | collective-permute-start | bytes 1376264 | tf_op jit(solution)/shard_map/ppermute | solution.py:37
  52.5 8.1 %collective-permute-start.9 = (bf16[256,896]{1,0:T(8,128)(2,1)}, bf16[256,896]{1,0:T(8,128)(2,1)}, u32[]{:S(2)}, u32[]{:S(2)}) collective-permute-start(bf16[256,896]{1,0:T(8,128)(2,1)} %slice.90), channel_id=1, source_target_pairs={{0,192},{64,0},{128,64},{192,128},{1,193},{65,1},{129,65},{193,129... | collective-permute-start | bytes 1376264 | tf_op jit(solution)/shard_map/ppermute | solution.py:37
  60.7 14.6 %collective-permute-start.16 = (bf16[256,896]{1,0:T(8,128)(2,1)S(1)}, bf16[256,896]{1,0:T(8,128)(2,1)S(1)}, u32[]{:S(2)}, u32[]{:S(2)}) collective-permute-start(bf16[256,896]{1,0:T(8,128)(2,1)S(1)} %collective-permute-done.7), channel_id=1, source_target_pairs={{0,48},{16,0},{32,16},{48,32},{1,49},{17,1},{33,17},{49,33},{2,50}... | collective-permute-start | bytes 1376264 | tf_op jit(solution)/shard_map/ppermute | solution.py:37
  64.5 31.0 %copy-start = (bf16[2048,896]{1,0:T(8,128)(2,1)}, bf16[2048,896]{1,0:T(8,128)(2,1)S(1)}, u32[]{:S(2)}) copy-start(bf16[2048,896]{1,0:T(8,128)(2,1)S(1)} %constant_dynamic-update-slice_fusion) | copy-start | bytes 11010052
  64.5 12.8 %collective-permute-start.18 = (bf16[2,4,32,1024]{3,2,0,1:T(8,128)(2,1)S(1)}, bf16[2,4,32,1024]{3,2,0,1:T(8,128)(2,1)S(1)}, u32[]{:S(2)}, u32[]{:S(2)}) collective-permute-start(bf16[2,4,32,1024]{3,2,0,1:T(8,128)(2,1)S(1)} %broadcast_select_fusion), channel_id=1, source_target_pairs={{0,8},{4,12},{8,0},{12,4},{1,9},{5,13},{9,1},{13,5},{2,10},{6,14},... | collective-permute-start | bytes 1572872 | tf_op jit(solution)/shard_map/ppermute | solution.py:37
  66.2 11.1 %collective-permute-start.19 = (bf16[3,2,4,32,1024]{4,3,1,2,0:T(8,128)(2,1)S(1)}, bf16[3,2,4,32,1024]{4,3,1,2,0:T(8,128)(2,1)S(1)}, u32[]{:S(2)}, u32[]{:S(2)}) collective-permute-start(bf16[3,2,4,32,1024]{4,3,1,2,0:T(8,128)(2,1)S(1)} %pad_maximum_fusion), channel_id=1, source_target_pairs={{0,1},{1,0},{2,3},{3,2},{4,5},{5,4},{6,7},{7,6},{8,9},{9,8},{10,11... | collective-permute-start | bytes 4718600 | tf_op jit(solution)/shard_map/ppermute | solution.py:37
  74.5 8.9 %collective-permute-start.12 = (bf16[1024,512]{1,0:T(8,128)(2,1)S(1)}, bf16[1024,512]{1,0:T(8,128)(2,1)S(1)}, u32[]{:S(2)}, u32[]{:S(2)}) collective-permute-start(bf16[1024,512]{1,0:T(8,128)(2,1)S(1)} %convolution_convert_fusion.1), channel_id=1, source_target_pairs={{0,1},{1,0},{2,3},{3,2},{4,5},{5,4},{6,7},{7,6},{8,9},{9,8},{10,11... | collective-permute-start | bytes 3145736 | tf_op jit(solution)/shard_map/ppermute | solution.py:37
  76.7 22.3 %collective-permute-start.17 = (bf16[1024,512]{1,0:T(8,128)(2,1)S(1)}, bf16[1024,512]{1,0:T(8,128)(2,1)S(1)}, u32[]{:S(2)}, u32[]{:S(2)}) collective-permute-start(bf16[1024,512]{1,0:T(8,128)(2,1)S(1)} %convolution_convert_fusion), channel_id=1, source_target_pairs={{0,1},{1,0},{2,3},{3,2},{4,5},{5,4},{6,7},{7,6},{8,9},{9,8},{10,11... | collective-permute-start | bytes 3145736 | tf_op jit(solution)/shard_map/ppermute | solution.py:37
  77.2 4.7 %collective-permute-start.20 = (bf16[2,4,32,1024]{3,2,0,1:T(8,128)(2,1)S(1)}, bf16[2,4,32,1024]{3,2,0,1:T(8,128)(2,1)S(1)}, u32[]{:S(2)}, u32[]{:S(2)}) collective-permute-start(bf16[2,4,32,1024]{3,2,0,1:T(8,128)(2,1)S(1)} %collective-permute-done.18), channel_id=1, source_target_pairs={{0,1},{1,0},{2,3},{3,2},{4,5},{5,4},{6,7},{7,6},{8,9},{9,8},{10,11... | collective-permute-start | bytes 1572872 | tf_op jit(solution)/shard_map/ppermute | solution.py:37
  83.3 12.2 %collective-permute-start.21 = (bf16[256,896]{1,0:T(8,128)(2,1)S(1)}, bf16[256,896]{1,0:T(8,128)(2,1)S(1)}, u32[]{:S(2)}, u32[]{:S(2)}) collective-permute-start(bf16[256,896]{1,0:T(8,128)(2,1)S(1)} %convolution_convert_fusion.2), channel_id=1, source_target_pairs={{0,48},{16,0},{32,16},{48,32},{1,49},{17,1},{33,17},{49,33},{2,50}... | collective-permute-start | bytes 1376264 | tf_op jit(solution)/shard_map/ppermute | solution.py:37
  84.9 16.9 %collective-permute-start.13 = (bf16[4,64,512]{2,1,0:T(8,128)(2,1)S(1)}, bf16[4,64,512]{2,1,0:T(8,128)(2,1)S(1)}, u32[]{:S(2)}, u32[]{:S(2)}) collective-permute-start(bf16[4,64,512]{2,1,0:T(8,128)(2,1)S(1)} %get-tuple-element.61), channel_id=1, source_target_pairs={{0,12},{4,0},{8,4},{12,8},{1,13},{5,1},{9,5},{13,9},{2,14},{6,2},{... | collective-permute-start | bytes 786440 | tf_op jit(solution)/shard_map/ppermute | solution.py:37
  86.5 15.4 %collective-permute-start.14 = (bf16[4,64,512]{2,1,0:T(8,128)(2,1)S(1)}, bf16[4,64,512]{2,1,0:T(8,128)(2,1)S(1)}, u32[]{:S(2)}, u32[]{:S(2)}) collective-permute-start(bf16[4,64,512]{2,1,0:T(8,128)(2,1)S(1)} %get-tuple-element.60), channel_id=1, source_target_pairs={{0,8},{4,12},{8,0},{12,4},{1,9},{5,13},{9,1},{13,5},{2,10},{6,14},... | collective-permute-start | bytes 786440 | tf_op jit(solution)/shard_map/ppermute | solution.py:37
  87.0 14.9 %collective-permute-start.15 = (bf16[4,64,512]{2,1,0:T(8,128)(2,1)S(1)}, bf16[4,64,512]{2,1,0:T(8,128)(2,1)S(1)}, u32[]{:S(2)}, u32[]{:S(2)}) collective-permute-start(bf16[4,64,512]{2,1,0:T(8,128)(2,1)S(1)} %get-tuple-element.59), channel_id=1, source_target_pairs={{0,4},{4,8},{8,12},{12,0},{1,5},{5,9},{9,13},{13,1},{2,6},{6,10},{... | collective-permute-start | bytes 786440 | tf_op jit(solution)/shard_map/ppermute | solution.py:37
  97.5 23.3 %collective-permute-start.22 = (bf16[256,896]{1,0:T(8,128)(2,1)}, bf16[256,896]{1,0:T(8,128)(2,1)}, u32[]{:S(2)}, u32[]{:S(2)}) collective-permute-start(bf16[256,896]{1,0:T(8,128)(2,1)} %add_convert_fusion.1), channel_id=1, source_target_pairs={{0,48},{16,0},{32,16},{48,32},{1,49},{17,1},{33,17},{49,33},{2,50}... | collective-permute-start | bytes 1376264 | tf_op jit(solution)/shard_map/ppermute | solution.py:37
  103.3 7.0 %collective-permute-start.23 = (bf16[4,64,512]{2,1,0:T(8,128)(2,1)}, bf16[4,64,512]{2,1,0:T(8,128)(2,1)}, u32[]{:S(2)}, u32[]{:S(2)}) collective-permute-start(bf16[4,64,512]{2,1,0:T(8,128)(2,1)} %get-tuple-element.43), channel_id=1, source_target_pairs={{0,12},{4,0},{8,4},{12,8},{1,13},{5,1},{9,5},{13,9},{2,14},{6,2},{... | collective-permute-start | bytes 786440 | tf_op jit(solution)/shard_map/ppermute | solution.py:37
  105.1 8.2 %collective-permute-start.24 = (bf16[4,64,512]{2,1,0:T(8,128)(2,1)}, bf16[4,64,512]{2,1,0:T(8,128)(2,1)}, u32[]{:S(2)}, u32[]{:S(2)}) collective-permute-start(bf16[4,64,512]{2,1,0:T(8,128)(2,1)} %get-tuple-element.44), channel_id=1, source_target_pairs={{0,8},{4,12},{8,0},{12,4},{1,9},{5,13},{9,1},{13,5},{2,10},{6,14},... | collective-permute-start | bytes 786440 | tf_op jit(solution)/shard_map/ppermute | solution.py:37
  105.6 15.1 %collective-permute-start.25 = (bf16[4,64,512]{2,1,0:T(8,128)(2,1)}, bf16[4,64,512]{2,1,0:T(8,128)(2,1)}, u32[]{:S(2)}, u32[]{:S(2)}) collective-permute-start(bf16[4,64,512]{2,1,0:T(8,128)(2,1)} %get-tuple-element.45), channel_id=1, source_target_pairs={{0,4},{4,8},{8,12},{12,0},{1,5},{5,9},{9,13},{13,1},{2,6},{6,10},{... | collective-permute-start | bytes 786440 | tf_op jit(solution)/shard_map/ppermute | solution.py:37
  122.3 17.4 %collective-permute-start.26 = (bf16[4,32,1024]{2,1,0:T(8,128)(2,1)S(1)}, bf16[4,32,1024]{2,1,0:T(8,128)(2,1)S(1)}, u32[]{:S(2)}, u32[]{:S(2)}) collective-permute-start(bf16[4,32,1024]{2,1,0:T(8,128)(2,1)S(1)} %fusion.15), channel_id=1, source_target_pairs={{0,2},{2,0},{1,3},{3,1},{4,6},{6,4},{5,7},{7,5},{8,10},{10,8},{9,1... | collective-permute-start | bytes 786440 | tf_op jit(solution)/shard_map/ppermute | solution.py:37
  126.4 22.1 %collective-permute-start.30 = (bf16[256,896]{1,0:T(8,128)(2,1)S(1)}, bf16[256,896]{1,0:T(8,128)(2,1)S(1)}, u32[]{:S(2)}, u32[]{:S(2)}) collective-permute-start(bf16[256,896]{1,0:T(8,128)(2,1)S(1)} %add_convert_fusion), channel_id=1, source_target_pairs={{0,48},{16,0},{32,16},{48,32},{1,49},{17,1},{33,17},{49,33},{2,50}... | collective-permute-start | bytes 1376264 | tf_op jit(solution)/shard_map/ppermute | solution.py:37
  139.9 4.8 %collective-permute-start.27 = (bf16[32,1024]{1,0:T(8,128)(2,1)S(1)}, bf16[32,1024]{1,0:T(8,128)(2,1)S(1)}, u32[]{:S(2)}, u32[]{:S(2)}) collective-permute-start(bf16[32,1024]{1,0:T(8,128)(2,1)S(1)} %get-tuple-element.68), channel_id=1, source_target_pairs={{0,192},{64,0},{128,64},{192,128},{1,193},{65,1},{129,65},{193,129... | collective-permute-start | bytes 196616 | tf_op jit(solution)/shard_map/ppermute | solution.py:37
  143.4 4.7 %collective-permute-start.28 = (bf16[32,1024]{1,0:T(8,128)(2,1)S(1)}, bf16[32,1024]{1,0:T(8,128)(2,1)S(1)}, u32[]{:S(2)}, u32[]{:S(2)}) collective-permute-start(bf16[32,1024]{1,0:T(8,128)(2,1)S(1)} %get-tuple-element.67), channel_id=1, source_target_pairs={{0,128},{64,192},{128,0},{192,64},{1,129},{65,193},{129,1},{193,65... | collective-permute-start | bytes 196616 | tf_op jit(solution)/shard_map/ppermute | solution.py:37
  143.4 5.0 %collective-permute-start.29 = (bf16[32,1024]{1,0:T(8,128)(2,1)S(1)}, bf16[32,1024]{1,0:T(8,128)(2,1)S(1)}, u32[]{:S(2)}, u32[]{:S(2)}) collective-permute-start(bf16[32,1024]{1,0:T(8,128)(2,1)S(1)} %get-tuple-element.66), channel_id=1, source_target_pairs={{0,64},{64,128},{128,192},{192,0},{1,65},{65,129},{129,193},{193,1... | collective-permute-start | bytes 196616 | tf_op jit(solution)/shard_map/ppermute | solution.py:37
  (15 other events, 107.1 us)
where the time goes:
time: 155 us; the launch traced here: 154 us
  waiting for transfers between devices  61.7 us (40%)
  starting transfers between devices  47.8 us (31%)
  local copies, waits for them, and re-layouts  20.9 us (13%)
  matrix products  13.7 us (9%)
  other arithmetic  8.17 us (5%)
    ppermute x31, waiting for transfers between devices, shift(): lax.ppermute(value, axis, [(i, (i + by) % size) for i in range(size)])  61.7 us
    ppermute x31, starting transfers between devices, shift(): lax.ppermute(value, axis, [(i, (i + by) % size) for i in range(size)])  47.8 us
    unnamed x36, local copies, waits for them, and re-layouts  9.2 us
    dot_general x4, matrix products, body(): lax.dot_general(scaled[:, m * depth:(m + 1) * depth], grads, (((0,), (0,)...  8.57 us
    slice x2, local copies, waits for them, and re-layouts, body(): far_a, far_b = (shift(below[:half], 'y', 1), shift(above[half:], 'y', -1))  3.65 us
  transfers between devices with their start and end apart: 31, of which 13 were waited for; matrix products, arithmetic and copies ran while one was open for 20% of the time, Pallas kernels for 0%

commit v1 on v0

--- a/solution.py
+++ b/solution.py
@@ -83,11 +83,14 @@
     other = shift(scaled, "zh", 1)
     masked_1 = shift(masked, "zl", -1)
     below, above = shift(own, "y", 1), shift(own, "y", -1)
-    other, masked_1, below, above = tie(other, masked_1, below, above)
+    below_half, above_half = below[:half], above[half:]
+    other, masked_1, below, above, below_half, above_half = tie(
+        other, masked_1, below, above, below_half, above_half
+    )
     scaled = in_place([scaled, other], jnp.where(zh == 0, jnp.arange(2), 1 - jnp.arange(2)))
 
     masked_2 = shift(masked_1, "zl", -1)
-    far_a, far_b = shift(below[:half], "y", 1), shift(above[half:], "y", -1)
+    far_a, far_b = shift(below_half, "y", 1), shift(above_half, "y", -1)
     scaled_1, scaled_3 = shift(scaled, "x", 1), shift(scaled, "x", 3)
     masked_2, far_a, far_b, scaled, scaled_1, scaled_3 = tie(
         masked_2, far_a, far_b, scaled, scaled_1, scaled_3

time: 155 us -> 154 us (level)
  transfers between devices with their start and end apart: 31 -> 31, of which waited for: 13 -> 16; matrix products, arithmetic and copies ran while one was open for 20% -> 20% of each run, Pallas kernels for 0% -> 0%
where the time goes in v1:
time: 154 us; the launch traced here: 153 us
  waiting for transfers between devices  61 us (40%)
  starting transfers between devices  47.2 us (31%)
  local copies, waits for them, and re-layouts  21.5 us (14%)
  matrix products  13.7 us (9%)
  other arithmetic  8.17 us (5%)
    ppermute x31, waiting for transfers between devices, shift(): lax.ppermute(value, axis, [(i, (i + by) % size) for i in range(size)])  61 us
    ppermute x31, starting transfers between devices, shift(): lax.ppermute(value, axis, [(i, (i + by) % size) for i in range(size)])  47.2 us
    unnamed x36, local copies, waits for them, and re-layouts  9.85 us
    dot_general x4, matrix products, body(): lax.dot_general(scaled[:, m * depth:(m + 1) * depth], grads, (((0,), (0,)...  8.57 us
    slice x2, local copies, waits for them, and re-layouts, body(): below_half, above_half = (below[:half], above[half:])  3.64 us
  transfers between devices with their start and end apart: 31, of which 16 were waited for; matrix products, arithmetic and copies ran while one was open for 20% of the time, Pallas kernels for 0%

profile of v1, /device:TPU:1, one launch (start us, length us, event | category | flops | bytes accessed | tf_op | source)
XLA Modules:
  0.0 153.0 jit_solution(1261136055870860534)
XLA Ops:
  2.2 3.6 %collective-permute-start.2 = (bf16[32,1024]{1,0:T(8,128)(2,1)S(1)}, bf16[32,1024]{1,0:T(8,128)(2,1)S(1)}, u32[]{:S(2)}, u32[]{:S(2)}) collective-permute-start(bf16[32,1024]{1,0:T(8,128)(2,1)S(1)} %pad_maximum_fusion.11), channel_id=1, source_target_pairs={{0,192},{64,0},{128,64},{192,128},{1,193},{65,1},{129,65},{193,129... | collective-permute-start | bytes 196616 | tf_op jit(solution)/shard_map/ppermute | solution.py:37
  6.9 2.2 %copy.25 = bf16[2,8,32,896]{3,2,1,0:T(8,128)(2,1)} copy(bf16[2,8,32,896]{3,2,0,1:T(8,128)(2,1)} %bitcast.159) | data formatting | bytes 1835008 | tf_op jit(solution)/shard_map/transpose | solution.py:59
  12.5 1.5 collective-permute-start.6
  16.2 4.4 %collective-permute-start.4 = (bf16[256,896]{1,0:T(8,128)(2,1)S(1)}, bf16[256,896]{1,0:T(8,128)(2,1)S(1)}, u32[]{:S(2)}, u32[]{:S(2)}) collective-permute-start(bf16[256,896]{1,0:T(8,128)(2,1)S(1)} %fusion.7), channel_id=1, source_target_pairs={{0,48},{16,0},{32,16},{48,32},{1,49},{17,1},{33,17},{49,33},{2,50}... | collective-permute-start | bytes 1376264 | tf_op jit(solution)/shard_map/ppermute | solution.py:37
  20.6 4.2 %collective-permute-start.3 = (bf16[4,32,1024]{2,1,0:T(8,128)(2,1)S(1)}, bf16[4,32,1024]{2,1,0:T(8,128)(2,1)S(1)}, u32[]{:S(2)}, u32[]{:S(2)}) collective-permute-start(bf16[4,32,1024]{2,1,0:T(8,128)(2,1)S(1)} %pad_maximum_fusion.8), channel_id=1, source_target_pairs={{0,2},{2,0},{1,3},{3,1},{4,6},{6,4},{5,7},{7,5},{8,10},{10,8},{9,1... | collective-permute-start | bytes 786440 | tf_op jit(solution)/shard_map/ppermute | solution.py:37
  24.8 7.8 %collective-permute-done.5 = bf16[512,896]{1,0:T(8,128)(2,1)} collective-permute-done((bf16[512,896]{1,0:T(8,128)(2,1)}, bf16[512,896]{1,0:T(8,128)(2,1)}, u32[]{:S(2)}, u32[]{:S(2)}) %collective-permute-start.5) | collective-permute-done | bytes 917536 | tf_op jit(solution)/shard_map/ppermute | solution.py:37
  32.6 1.8 %slice.112 = bf16[256,896]{1,0:T(8,128)(2,1)} slice(bf16[512,896]{1,0:T(8,128)(2,1)} %collective-permute-done.5), slice={[0:256], [0:896]} | slice | bytes 917504 | tf_op jit(solution)/shard_map/slice | solution.py:86
  34.4 1.8 %slice.113 = bf16[256,896]{1,0:T(8,128)(2,1)} slice(bf16[512,896]{1,0:T(8,128)(2,1)} %collective-permute-done.6), slice={[256:512], [0:896]} | slice | bytes 917504 | tf_op jit(solution)/shard_map/slice | solution.py:86
  36.2 7.5 %collective-permute-done.3 = bf16[4,32,1024]{2,1,0:T(8,128)(2,1)S(1)} collective-permute-done((bf16[4,32,1024]{2,1,0:T(8,128)(2,1)S(1)}, bf16[4,32,1024]{2,1,0:T(8,128)(2,1)S(1)}, u32[]{:S(2)}, u32[]{:S(2)}) %collective-permute-start.3) | collective-permute-done | bytes 262176 | tf_op jit(solution)/shard_map/ppermute | solution.py:37
  45.9 1.5 collective-permute-start.11
  48.9 1.7 %collective-permute-start.9 = (bf16[256,896]{1,0:T(8,128)(2,1)}, bf16[256,896]{1,0:T(8,128)(2,1)}, u32[]{:S(2)}, u32[]{:S(2)}) collective-permute-start(bf16[256,896]{1,0:T(8,128)(2,1)} %slice.113), channel_id=1, source_target_pairs={{0,192},{64,0},{128,64},{192,128},{1,193},{65,1},{129,65},{193,129... | collective-permute-start | bytes 1376264 | tf_op jit(solution)/shard_map/ppermute | solution.py:37
  51.8 1.3 constant_dynamic-update-slice_fusion.3
  53.1 2.0 %collective-permute-done.7 = bf16[256,896]{1,0:T(8,128)(2,1)S(1)} collective-permute-done((bf16[256,896]{1,0:T(8,128)(2,1)}, bf16[256,896]{1,0:T(8,128)(2,1)S(1)}, u32[]{:S(2)}, u32[]{:S(2)}) %collective-permute-start.7) | collective-permute-done | bytes 458784 | tf_op jit(solution)/shard_map/ppermute | solution.py:37
  55.2 1.8 %collective-permute-done.8 = bf16[256,896]{1,0:T(8,128)(2,1)} collective-permute-done((bf16[256,896]{1,0:T(8,128)(2,1)}, bf16[256,896]{1,0:T(8,128)(2,1)}, u32[]{:S(2)}, u32[]{:S(2)}) %collective-permute-start.8) | collective-permute-done | bytes 458784 | tf_op jit(solution)/shard_map/ppermute | solution.py:37
  57.1 1.6 %collective-permute-start.18 = (bf16[2,4,32,1024]{3,2,0,1:T(8,128)(2,1)S(1)}, bf16[2,4,32,1024]{3,2,0,1:T(8,128)(2,1)S(1)}, u32[]{:S(2)}, u32[]{:S(2)}) collective-permute-start(bf16[2,4,32,1024]{3,2,0,1:T(8,128)(2,1)S(1)} %broadcast_select_fusion), channel_id=1, source_target_pairs={{0,8},{4,12},{8,0},{12,4},{1,9},{5,13},{9,1},{13,5},{2,10},{6,14},... | collective-permute-start | bytes 1572872 | tf_op jit(solution)/shard_map/ppermute | solution.py:37
  58.9 6.2 %collective-permute-start.19 = (bf16[3,2,4,32,1024]{4,3,1,2,0:T(8,128)(2,1)S(1)}, bf16[3,2,4,32,1024]{4,3,1,2,0:T(8,128)(2,1)S(1)}, u32[]{:S(2)}, u32[]{:S(2)}) collective-permute-start(bf16[3,2,4,32,1024]{4,3,1,2,0:T(8,128)(2,1)S(1)} %pad_maximum_fusion), channel_id=1, source_target_pairs={{0,1},{1,0},{2,3},{3,2},{4,5},{5,4},{6,7},{7,6},{8,9},{9,8},{10,11... | collective-permute-start | bytes 4718600 | tf_op jit(solution)/shard_map/ppermute | solution.py:37
  73.1 4.1 %collective-permute-done.16 = bf16[256,896]{1,0:T(8,128)(2,1)S(1)} collective-permute-done((bf16[256,896]{1,0:T(8,128)(2,1)S(1)}, bf16[256,896]{1,0:T(8,128)(2,1)S(1)}, u32[]{:S(2)}, u32[]{:S(2)}) %collective-permute-start.16) | collective-permute-done | bytes 458784 | tf_op jit(solution)/shard_map/ppermute | solution.py:37
  79.8 2.7 %collective-permute-done.20 = bf16[2,4,32,1024]{3,2,0,1:T(8,128)(2,1)S(1)} collective-permute-done((bf16[2,4,32,1024]{3,2,0,1:T(8,128)(2,1)S(1)}, bf16[2,4,32,1024]{3,2,0,1:T(8,128)(2,1)S(1)}, u32[]{:S(2)}, u32[]{:S(2)}) %collective-permute-start.20) | collective-permute-done | bytes 524320 | tf_op jit(solution)/shard_map/ppermute | solution.py:37
  83.8 2.1 %collective-permute-start.21 = (bf16[256,896]{1,0:T(8,128)(2,1)S(1)}, bf16[256,896]{1,0:T(8,128)(2,1)S(1)}, u32[]{:S(2)}, u32[]{:S(2)}) collective-permute-start(bf16[256,896]{1,0:T(8,128)(2,1)S(1)} %convolution_convert_fusion.2), channel_id=1, source_target_pairs={{0,48},{16,0},{32,16},{48,32},{1,49},{17,1},{33,17},{49,33},{2,50}... | collective-permute-start | bytes 1376264 | tf_op jit(solution)/shard_map/ppermute | solution.py:37
  89.8 5.8 %collective-permute-done.21 = bf16[256,896]{1,0:T(8,128)(2,1)S(1)} collective-permute-done((bf16[256,896]{1,0:T(8,128)(2,1)S(1)}, bf16[256,896]{1,0:T(8,128)(2,1)S(1)}, u32[]{:S(2)}, u32[]{:S(2)}) %collective-permute-start.21) | collective-permute-done | bytes 458784 | tf_op jit(solution)/shard_map/ppermute | solution.py:37
  95.7 2.1 %add_convert_fusion.1 = bf16[256,896]{1,0:T(8,128)(2,1)} fusion(bf16[256,896]{1,0:T(8,128)(2,1)S(1)} %collective-permute-done.21, bf16[2048,896]{1,0:T(8,128)(2,1)S(1)} %constant_dynamic-update-slice_fusion, bf16[2048,1024]{1,0:T(8,128)(2,1)S(1)} %bitcast.144), kind=kOutput, calls=%fused_computation.23 | convolution fusion | flops 940212224 | bytes 5636096 | tf_op jit(solution)/shard_map/dot_general | solution.py:122
  97.7 3.8 %collective-permute-start.22 = (bf16[256,896]{1,0:T(8,128)(2,1)}, bf16[256,896]{1,0:T(8,128)(2,1)}, u32[]{:S(2)}, u32[]{:S(2)}) collective-permute-start(bf16[256,896]{1,0:T(8,128)(2,1)} %add_convert_fusion.1), channel_id=1, source_target_pairs={{0,48},{16,0},{32,16},{48,32},{1,49},{17,1},{33,17},{49,33},{2,50}... | collective-permute-start | bytes 1376264 | tf_op jit(solution)/shard_map/ppermute | solution.py:37
  109.4 3.1 %collective-permute-done.23 = bf16[4,64,512]{2,1,0:T(8,128)(2,1)} collective-permute-done((bf16[4,64,512]{2,1,0:T(8,128)(2,1)}, bf16[4,64,512]{2,1,0:T(8,128)(2,1)}, u32[]{:S(2)}, u32[]{:S(2)}) %collective-permute-start.23) | collective-permute-done | bytes 262176 | tf_op jit(solution)/shard_map/ppermute | solution.py:37
  112.5 2.1 %collective-permute-done.24 = bf16[4,64,512]{2,1,0:T(8,128)(2,1)} collective-permute-done((bf16[4,64,512]{2,1,0:T(8,128)(2,1)}, bf16[4,64,512]{2,1,0:T(8,128)(2,1)}, u32[]{:S(2)}, u32[]{:S(2)}) %collective-permute-start.24) | collective-permute-done | bytes 262176 | tf_op jit(solution)/shard_map/ppermute | solution.py:37
  114.6 7.8 %collective-permute-done.25 = bf16[4,64,512]{2,1,0:T(8,128)(2,1)} collective-permute-done((bf16[4,64,512]{2,1,0:T(8,128)(2,1)}, bf16[4,64,512]{2,1,0:T(8,128)(2,1)}, u32[]{:S(2)}, u32[]{:S(2)}) %collective-permute-start.25) | collective-permute-done | bytes 262176 | tf_op jit(solution)/shard_map/ppermute | solution.py:37
  122.3 1.4 fusion.11
  123.9 1.8 %collective-permute-start.26 = (bf16[4,32,1024]{2,1,0:T(8,128)(2,1)S(1)}, bf16[4,32,1024]{2,1,0:T(8,128)(2,1)S(1)}, u32[]{:S(2)}, u32[]{:S(2)}) collective-permute-start(bf16[4,32,1024]{2,1,0:T(8,128)(2,1)S(1)} %fusion.15), channel_id=1, source_target_pairs={{0,2},{2,0},{1,3},{3,1},{4,6},{6,4},{5,7},{7,5},{8,10},{10,8},{9,1... | collective-permute-start | bytes 786440 | tf_op jit(solution)/shard_map/ppermute | solution.py:37
  125.7 2.6 %add_convert_fusion = bf16[256,896]{1,0:T(8,128)(2,1)S(1)} fusion(bf16[256,896]{1,0:T(8,128)(2,1)} %collective-permute-done.22, bf16[2048,896]{1,0:T(8,128)(2,1)S(1)} %copy-done.1, bf16[2048,1024]{1,0:T(8,128)(2,1)} %bitcast.145), kind=kOutput, calls=%fused_computation.22 | convolution fusion | flops 940212224 | bytes 5636096 | tf_op jit(solution)/shard_map/dot_general | solution.py:122
  128.4 11.2 %collective-permute-done.26 = bf16[4,32,1024]{2,1,0:T(8,128)(2,1)S(1)} collective-permute-done((bf16[4,32,1024]{2,1,0:T(8,128)(2,1)S(1)}, bf16[4,32,1024]{2,1,0:T(8,128)(2,1)S(1)}, u32[]{:S(2)}, u32[]{:S(2)}) %collective-permute-start.26) | collective-permute-done | bytes 262176 | tf_op jit(solution)/shard_map/ppermute | solution.py:37
  139.9 2.5 %collective-permute-start.27 = (bf16[32,1024]{1,0:T(8,128)(2,1)S(1)}, bf16[32,1024]{1,0:T(8,128)(2,1)S(1)}, u32[]{:S(2)}, u32[]{:S(2)}) collective-permute-start(bf16[32,1024]{1,0:T(8,128)(2,1)S(1)} %get-tuple-element.72), channel_id=1, source_target_pairs={{0,192},{64,0},{128,64},{192,128},{1,193},{65,1},{129,65},{193,129... | collective-permute-start | bytes 196616 | tf_op jit(solution)/shard_map/ppermute | solution.py:37
  143.7 3.4 %collective-permute-done.28 = bf16[32,1024]{1,0:T(8,128)(2,1)S(1)} collective-permute-done((bf16[32,1024]{1,0:T(8,128)(2,1)S(1)}, bf16[32,1024]{1,0:T(8,128)(2,1)S(1)}, u32[]{:S(2)}, u32[]{:S(2)}) %collective-permute-start.28) | collective-permute-done | bytes 65568 | tf_op jit(solution)/shard_map/ppermute | solution.py:37
  147.8 2.6 %convert_multiply_fusion = f32[256,896]{1,0:T(8,128)S(1)} fusion(bf16[256,896]{1,0:T(8,128)(2,1)S(1)} %copy-done.7, bf16[256,896]{1,0:T(8,128)(2,1)S(1)} %collective-permute-done.30, bf16[2048,896]{1,0:T(8,128)(2,1)S(1)} %copy-done.1, bf16[2048,1024]{1,0:T(8,128)(2,1)} %bitcast.146), kind=kOutput, calls=%fused_computation.9 | convolution fusion | flops 940441600 | bytes 6553600 | tf_op jit(solution)/shard_map/dot_general | solution.py:122
  (132 shorter events, 41.7 us)
Async XLA Ops:
  2.2 8.5 %collective-permute-start.2 = (bf16[32,1024]{1,0:T(8,128)(2,1)S(1)}, bf16[32,1024]{1,0:T(8,128)(2,1)S(1)}, u32[]{:S(2)}, u32[]{:S(2)}) collective-permute-start(bf16[32,1024]{1,0:T(8,128)(2,1)S(1)} %pad_maximum_fusion.11), channel_id=1, source_target_pairs={{0,192},{64,0},{128,64},{192,128},{1,193},{65,1},{129,65},{193,129... | collective-permute-start | bytes 196616 | tf_op jit(solution)/shard_map/ppermute | solution.py:37
  5.9 4.9 %collective-permute-start.1 = (bf16[32,1024]{1,0:T(8,128)(2,1)S(1)}, bf16[32,1024]{1,0:T(8,128)(2,1)S(1)}, u32[]{:S(2)}, u32[]{:S(2)}) collective-permute-start(bf16[32,1024]{1,0:T(8,128)(2,1)S(1)} %pad_maximum_fusion.10), channel_id=1, source_target_pairs={{0,128},{64,192},{128,0},{192,64},{1,129},{65,193},{129,1},{193,65... | collective-permute-start | bytes 196616 | tf_op jit(solution)/shard_map/ppermute | solution.py:37
  6.2 5.0 %collective-permute-start = (bf16[32,1024]{1,0:T(8,128)(2,1)S(1)}, bf16[32,1024]{1,0:T(8,128)(2,1)S(1)}, u32[]{:S(2)}, u32[]{:S(2)}) collective-permute-start(bf16[32,1024]{1,0:T(8,128)(2,1)S(1)} %pad_maximum_fusion.9), channel_id=1, source_target_pairs={{0,64},{64,128},{128,192},{192,0},{1,65},{65,129},{129,193},{193,1... | collective-permute-start | bytes 196616 | tf_op jit(solution)/shard_map/ppermute | solution.py:37
  11.2 21.3 %collective-permute-start.5 = (bf16[512,896]{1,0:T(8,128)(2,1)}, bf16[512,896]{1,0:T(8,128)(2,1)}, u32[]{:S(2)}, u32[]{:S(2)}) collective-permute-start(bf16[512,896]{1,0:T(8,128)(2,1)} %bitcast.6), channel_id=1, source_target_pairs={{0,64},{64,128},{128,192},{192,0},{1,65},{65,129},{129,193},{193,1... | collective-permute-start | bytes 2752520 | tf_op jit(solution)/shard_map/ppermute | solution.py:37
  12.5 21.9 %collective-permute-start.6 = (bf16[512,896]{1,0:T(8,128)(2,1)}, bf16[512,896]{1,0:T(8,128)(2,1)}, u32[]{:S(2)}, u32[]{:S(2)}) collective-permute-start(bf16[512,896]{1,0:T(8,128)(2,1)} %bitcast.6), channel_id=1, source_target_pairs={{0,192},{64,0},{128,64},{192,128},{1,193},{65,1},{129,65},{193,129... | collective-permute-start | bytes 2752520 | tf_op jit(solution)/shard_map/ppermute | solution.py:37
  16.2 27.6 %copy-start.8 = (bf16[256,896]{1,0:T(8,128)(2,1)}, bf16[256,896]{1,0:T(8,128)(2,1)S(1)}, u32[]{:S(2)}) copy-start(bf16[256,896]{1,0:T(8,128)(2,1)S(1)} %fusion.7) | copy-start | bytes 1376260
  16.2 27.5 %collective-permute-start.4 = (bf16[256,896]{1,0:T(8,128)(2,1)S(1)}, bf16[256,896]{1,0:T(8,128)(2,1)S(1)}, u32[]{:S(2)}, u32[]{:S(2)}) collective-permute-start(bf16[256,896]{1,0:T(8,128)(2,1)S(1)} %fusion.7), channel_id=1, source_target_pairs={{0,48},{16,0},{32,16},{48,32},{1,49},{17,1},{33,17},{49,33},{2,50}... | collective-permute-start | bytes 1376264 | tf_op jit(solution)/shard_map/ppermute | solution.py:37
  20.6 23.1 %collective-permute-start.3 = (bf16[4,32,1024]{2,1,0:T(8,128)(2,1)S(1)}, bf16[4,32,1024]{2,1,0:T(8,128)(2,1)S(1)}, u32[]{:S(2)}, u32[]{:S(2)}) collective-permute-start(bf16[4,32,1024]{2,1,0:T(8,128)(2,1)S(1)} %pad_maximum_fusion.8), channel_id=1, source_target_pairs={{0,2},{2,0},{1,3},{3,1},{4,6},{6,4},{5,7},{7,5},{8,10},{10,8},{9,1... | collective-permute-start | bytes 786440 | tf_op jit(solution)/shard_map/ppermute | solution.py:37
  44.6 12.5 %collective-permute-start.10 = (bf16[2,4,32,1024]{3,2,0,1:T(8,128)(2,1)S(1)}, bf16[2,4,32,1024]{3,2,0,1:T(8,128)(2,1)S(1)}, u32[]{:S(2)}, u32[]{:S(2)}) collective-permute-start(bf16[2,4,32,1024]{3,2,0,1:T(8,128)(2,1)S(1)} %broadcast_select_fusion), channel_id=1, source_target_pairs={{0,4},{4,8},{8,12},{12,0},{1,5},{5,9},{9,13},{13,1},{2,6},{6,10},{... | collective-permute-start | bytes 1572872 | tf_op jit(solution)/shard_map/ppermute | solution.py:37
  45.9 11.2 %collective-permute-start.11 = (bf16[2,4,32,1024]{3,2,0,1:T(8,128)(2,1)S(1)}, bf16[2,4,32,1024]{3,2,0,1:T(8,128)(2,1)S(1)}, u32[]{:S(2)}, u32[]{:S(2)}) collective-permute-start(bf16[2,4,32,1024]{3,2,0,1:T(8,128)(2,1)S(1)} %broadcast_select_fusion), channel_id=1, source_target_pairs={{0,12},{4,0},{8,4},{12,8},{1,13},{5,1},{9,5},{13,9},{2,14},{6,2},{... | collective-permute-start | bytes 1572872 | tf_op jit(solution)/shard_map/ppermute | solution.py:37
  47.4 7.8 %collective-permute-start.7 = (bf16[256,896]{1,0:T(8,128)(2,1)}, bf16[256,896]{1,0:T(8,128)(2,1)S(1)}, u32[]{:S(2)}, u32[]{:S(2)}) collective-permute-start(bf16[256,896]{1,0:T(8,128)(2,1)} %copy-done.14), channel_id=1, source_target_pairs={{0,48},{16,0},{32,16},{48,32},{1,49},{17,1},{33,17},{49,33},{2,50}... | collective-permute-start | bytes 1376264 | tf_op jit(solution)/shard_map/ppermute | solution.py:37
  47.9 9.0 %collective-permute-start.8 = (bf16[256,896]{1,0:T(8,128)(2,1)}, bf16[256,896]{1,0:T(8,128)(2,1)}, u32[]{:S(2)}, u32[]{:S(2)}) collective-permute-start(bf16[256,896]{1,0:T(8,128)(2,1)} %slice.112), channel_id=1, source_target_pairs={{0,64},{64,128},{128,192},{192,0},{1,65},{65,129},{129,193},{193,1... | collective-permute-start | bytes 1376264 | tf_op jit(solution)/shard_map/ppermute | solution.py:37
  48.9 8.2 %collective-permute-start.9 = (bf16[256,896]{1,0:T(8,128)(2,1)}, bf16[256,896]{1,0:T(8,128)(2,1)}, u32[]{:S(2)}, u32[]{:S(2)}) collective-permute-start(bf16[256,896]{1,0:T(8,128)(2,1)} %slice.113), channel_id=1, source_target_pairs={{0,192},{64,0},{128,64},{192,128},{1,193},{65,1},{129,65},{193,129... | collective-permute-start | bytes 1376264 | tf_op jit(solution)/shard_map/ppermute | solution.py:37
  57.1 22.4 %collective-permute-start.18 = (bf16[2,4,32,1024]{3,2,0,1:T(8,128)(2,1)S(1)}, bf16[2,4,32,1024]{3,2,0,1:T(8,128)(2,1)S(1)}, u32[]{:S(2)}, u32[]{:S(2)}) collective-permute-start(bf16[2,4,32,1024]{3,2,0,1:T(8,128)(2,1)S(1)} %broadcast_select_fusion), channel_id=1, source_target_pairs={{0,8},{4,12},{8,0},{12,4},{1,9},{5,13},{9,1},{13,5},{2,10},{6,14},... | collective-permute-start | bytes 1572872 | tf_op jit(solution)/shard_map/ppermute | solution.py:37
  58.9 20.6 %collective-permute-start.19 = (bf16[3,2,4,32,1024]{4,3,1,2,0:T(8,128)(2,1)S(1)}, bf16[3,2,4,32,1024]{4,3,1,2,0:T(8,128)(2,1)S(1)}, u32[]{:S(2)}, u32[]{:S(2)}) collective-permute-start(bf16[3,2,4,32,1024]{4,3,1,2,0:T(8,128)(2,1)S(1)} %pad_maximum_fusion), channel_id=1, source_target_pairs={{0,1},{1,0},{2,3},{3,2},{4,5},{5,4},{6,7},{7,6},{8,9},{9,8},{10,11... | collective-permute-start | bytes 4718600 | tf_op jit(solution)/shard_map/ppermute | solution.py:37
  65.1 12.1 %collective-permute-start.16 = (bf16[256,896]{1,0:T(8,128)(2,1)S(1)}, bf16[256,896]{1,0:T(8,128)(2,1)S(1)}, u32[]{:S(2)}, u32[]{:S(2)}) collective-permute-start(bf16[256,896]{1,0:T(8,128)(2,1)S(1)} %collective-permute-done.7), channel_id=1, source_target_pairs={{0,48},{16,0},{32,16},{48,32},{1,49},{17,1},{33,17},{49,33},{2,50}... | collective-permute-start | bytes 1376264 | tf_op jit(solution)/shard_map/ppermute | solution.py:37
  71.9 14.0 %collective-permute-start.12 = (bf16[1024,512]{1,0:T(8,128)(2,1)S(1)}, bf16[1024,512]{1,0:T(8,128)(2,1)S(1)}, u32[]{:S(2)}, u32[]{:S(2)}) collective-permute-start(bf16[1024,512]{1,0:T(8,128)(2,1)S(1)} %convolution_convert_fusion.1), channel_id=1, source_target_pairs={{0,1},{1,0},{2,3},{3,2},{4,5},{5,4},{6,7},{7,6},{8,9},{9,8},{10,11... | collective-permute-start | bytes 3145736 | tf_op jit(solution)/shard_map/ppermute | solution.py:37
  78.5 23.0 %collective-permute-start.17 = (bf16[1024,512]{1,0:T(8,128)(2,1)S(1)}, bf16[1024,512]{1,0:T(8,128)(2,1)S(1)}, u32[]{:S(2)}, u32[]{:S(2)}) collective-permute-start(bf16[1024,512]{1,0:T(8,128)(2,1)S(1)} %convolution_convert_fusion), channel_id=1, source_target_pairs={{0,1},{1,0},{2,3},{3,2},{4,5},{5,4},{6,7},{7,6},{8,9},{9,8},{10,11... | collective-permute-start | bytes 3145736 | tf_op jit(solution)/shard_map/ppermute | solution.py:37
  79.5 3.0 %collective-permute-start.20 = (bf16[2,4,32,1024]{3,2,0,1:T(8,128)(2,1)S(1)}, bf16[2,4,32,1024]{3,2,0,1:T(8,128)(2,1)S(1)}, u32[]{:S(2)}, u32[]{:S(2)}) collective-permute-start(bf16[2,4,32,1024]{3,2,0,1:T(8,128)(2,1)S(1)} %collective-permute-done.18), channel_id=1, source_target_pairs={{0,1},{1,0},{2,3},{3,2},{4,5},{5,4},{6,7},{7,6},{8,9},{9,8},{10,11... | collective-permute-start | bytes 1572872 | tf_op jit(solution)/shard_map/ppermute | solution.py:37
  83.8 11.8 %collective-permute-start.21 = (bf16[256,896]{1,0:T(8,128)(2,1)S(1)}, bf16[256,896]{1,0:T(8,128)(2,1)S(1)}, u32[]{:S(2)}, u32[]{:S(2)}) collective-permute-start(bf16[256,896]{1,0:T(8,128)(2,1)S(1)} %convolution_convert_fusion.2), channel_id=1, source_target_pairs={{0,48},{16,0},{32,16},{48,32},{1,49},{17,1},{33,17},{49,33},{2,50}... | collective-permute-start | bytes 1376264 | tf_op jit(solution)/shard_map/ppermute | solution.py:37
  87.4 17.0 %collective-permute-start.13 = (bf16[4,64,512]{2,1,0:T(8,128)(2,1)S(1)}, bf16[4,64,512]{2,1,0:T(8,128)(2,1)S(1)}, u32[]{:S(2)}, u32[]{:S(2)}) collective-permute-start(bf16[4,64,512]{2,1,0:T(8,128)(2,1)S(1)} %get-tuple-element.65), channel_id=1, source_target_pairs={{0,12},{4,0},{8,4},{12,8},{1,13},{5,1},{9,5},{13,9},{2,14},{6,2},{... | collective-permute-start | bytes 786440 | tf_op jit(solution)/shard_map/ppermute | solution.py:37
  88.4 16.0 %collective-permute-start.14 = (bf16[4,64,512]{2,1,0:T(8,128)(2,1)S(1)}, bf16[4,64,512]{2,1,0:T(8,128)(2,1)S(1)}, u32[]{:S(2)}, u32[]{:S(2)}) collective-permute-start(bf16[4,64,512]{2,1,0:T(8,128)(2,1)S(1)} %get-tuple-element.64), channel_id=1, source_target_pairs={{0,8},{4,12},{8,0},{12,4},{1,9},{5,13},{9,1},{13,5},{2,10},{6,14},... | collective-permute-start | bytes 786440 | tf_op jit(solution)/shard_map/ppermute | solution.py:37
  89.6 14.8 %collective-permute-start.15 = (bf16[4,64,512]{2,1,0:T(8,128)(2,1)S(1)}, bf16[4,64,512]{2,1,0:T(8,128)(2,1)S(1)}, u32[]{:S(2)}, u32[]{:S(2)}) collective-permute-start(bf16[4,64,512]{2,1,0:T(8,128)(2,1)S(1)} %get-tuple-element.63), channel_id=1, source_target_pairs={{0,4},{4,8},{8,12},{12,0},{1,5},{5,9},{9,13},{13,1},{2,6},{6,10},{... | collective-permute-start | bytes 786440 | tf_op jit(solution)/shard_map/ppermute | solution.py:37
  97.7 24.6 %collective-permute-start.22 = (bf16[256,896]{1,0:T(8,128)(2,1)}, bf16[256,896]{1,0:T(8,128)(2,1)}, u32[]{:S(2)}, u32[]{:S(2)}) collective-permute-start(bf16[256,896]{1,0:T(8,128)(2,1)} %add_convert_fusion.1), channel_id=1, source_target_pairs={{0,48},{16,0},{32,16},{48,32},{1,49},{17,1},{33,17},{49,33},{2,50}... | collective-permute-start | bytes 1376264 | tf_op jit(solution)/shard_map/ppermute | solution.py:37
  105.8 6.6 %collective-permute-start.23 = (bf16[4,64,512]{2,1,0:T(8,128)(2,1)}, bf16[4,64,512]{2,1,0:T(8,128)(2,1)}, u32[]{:S(2)}, u32[]{:S(2)}) collective-permute-start(bf16[4,64,512]{2,1,0:T(8,128)(2,1)} %get-tuple-element.47), channel_id=1, source_target_pairs={{0,12},{4,0},{8,4},{12,8},{1,13},{5,1},{9,5},{13,9},{2,14},{6,2},{... | collective-permute-start | bytes 786440 | tf_op jit(solution)/shard_map/ppermute | solution.py:37
  106.7 7.9 %collective-permute-start.24 = (bf16[4,64,512]{2,1,0:T(8,128)(2,1)}, bf16[4,64,512]{2,1,0:T(8,128)(2,1)}, u32[]{:S(2)}, u32[]{:S(2)}) collective-permute-start(bf16[4,64,512]{2,1,0:T(8,128)(2,1)} %get-tuple-element.48), channel_id=1, source_target_pairs={{0,8},{4,12},{8,0},{12,4},{1,9},{5,13},{9,1},{13,5},{2,10},{6,14},... | collective-permute-start | bytes 786440 | tf_op jit(solution)/shard_map/ppermute | solution.py:37
  107.9 14.4 %collective-permute-start.25 = (bf16[4,64,512]{2,1,0:T(8,128)(2,1)}, bf16[4,64,512]{2,1,0:T(8,128)(2,1)}, u32[]{:S(2)}, u32[]{:S(2)}) collective-permute-start(bf16[4,64,512]{2,1,0:T(8,128)(2,1)} %get-tuple-element.49), channel_id=1, source_target_pairs={{0,4},{4,8},{8,12},{12,0},{1,5},{5,9},{9,13},{13,1},{2,6},{6,10},{... | collective-permute-start | bytes 786440 | tf_op jit(solution)/shard_map/ppermute | solution.py:37
  123.9 15.7 %collective-permute-start.26 = (bf16[4,32,1024]{2,1,0:T(8,128)(2,1)S(1)}, bf16[4,32,1024]{2,1,0:T(8,128)(2,1)S(1)}, u32[]{:S(2)}, u32[]{:S(2)}) collective-permute-start(bf16[4,32,1024]{2,1,0:T(8,128)(2,1)S(1)} %fusion.15), channel_id=1, source_target_pairs={{0,2},{2,0},{1,3},{3,1},{4,6},{6,4},{5,7},{7,5},{8,10},{10,8},{9,1... | collective-permute-start | bytes 786440 | tf_op jit(solution)/shard_map/ppermute | solution.py:37
  128.4 19.4 %collective-permute-start.30 = (bf16[256,896]{1,0:T(8,128)(2,1)S(1)}, bf16[256,896]{1,0:T(8,128)(2,1)S(1)}, u32[]{:S(2)}, u32[]{:S(2)}) collective-permute-start(bf16[256,896]{1,0:T(8,128)(2,1)S(1)} %add_convert_fusion), channel_id=1, source_target_pairs={{0,48},{16,0},{32,16},{48,32},{1,49},{17,1},{33,17},{49,33},{2,50}... | collective-permute-start | bytes 1376264 | tf_op jit(solution)/shard_map/ppermute | solution.py:37
  139.9 3.8 %collective-permute-start.27 = (bf16[32,1024]{1,0:T(8,128)(2,1)S(1)}, bf16[32,1024]{1,0:T(8,128)(2,1)S(1)}, u32[]{:S(2)}, u32[]{:S(2)}) collective-permute-start(bf16[32,1024]{1,0:T(8,128)(2,1)S(1)} %get-tuple-element.72), channel_id=1, source_target_pairs={{0,192},{64,0},{128,64},{192,128},{1,193},{65,1},{129,65},{193,129... | collective-permute-start | bytes 196616 | tf_op jit(solution)/shard_map/ppermute | solution.py:37
  142.4 4.7 %collective-permute-start.28 = (bf16[32,1024]{1,0:T(8,128)(2,1)S(1)}, bf16[32,1024]{1,0:T(8,128)(2,1)S(1)}, u32[]{:S(2)}, u32[]{:S(2)}) collective-permute-start(bf16[32,1024]{1,0:T(8,128)(2,1)S(1)} %get-tuple-element.71), channel_id=1, source_target_pairs={{0,128},{64,192},{128,0},{192,64},{1,129},{65,193},{129,1},{193,65... | collective-permute-start | bytes 196616 | tf_op jit(solution)/shard_map/ppermute | solution.py:37
  142.4 5.4 %collective-permute-start.29 = (bf16[32,1024]{1,0:T(8,128)(2,1)S(1)}, bf16[32,1024]{1,0:T(8,128)(2,1)S(1)}, u32[]{:S(2)}, u32[]{:S(2)}) collective-permute-start(bf16[32,1024]{1,0:T(8,128)(2,1)S(1)} %get-tuple-element.70), channel_id=1, source_target_pairs={{0,64},{64,128},{128,192},{192,0},{1,65},{65,129},{129,193},{193,1... | collective-permute-start | bytes 196616 | tf_op jit(solution)/shard_map/ppermute | solution.py:37
  (15 other events, 104.4 us)

commit v2 on v1

--- a/solution.py
+++ b/solution.py
@@ -128,6 +128,7 @@
         for m in range(4)
     ]
     moving = grad_w[1].astype(BF16)
+    moving, masked_3 = tie(moving, masked_3)
 
     grads = grads.reshape(4, 2, half, hidden)
     mine = lax.dynamic_index_in_dim(grads, core, 1, False).reshape(4 * half, hidden)

time: 154 us -> 150 us (0.974)
  waiting for transfers between devices: 61 us -> 56.4 us
    ppermute x31, waiting for transfers between devices: 61 us -> 56.4 us  [shift(): lax.ppermute(value, axis, [(i, (i + by) % size) for i in range(size)])]
  transfers between devices with their start and end apart: 31 -> 31, of which waited for: 16 -> 15; matrix products, arithmetic and copies ran while one was open for 20% -> 20% of each run, Pallas kernels for 0% -> 0%
where the time goes in v2:
time: 150 us; the launch traced here: 149 us
  waiting for transfers between devices  56.4 us (38%)
  starting transfers between devices  47.9 us (32%)
  local copies, waits for them, and re-layouts  21.5 us (14%)
  matrix products  13.7 us (9%)
  other arithmetic  8.17 us (5%)
    ppermute x31, waiting for transfers between devices, shift(): lax.ppermute(value, axis, [(i, (i + by) % size) for i in range(size)])  56.4 us
    ppermute x31, starting transfers between devices, shift(): lax.ppermute(value, axis, [(i, (i + by) % size) for i in range(size)])  47.9 us
    unnamed x36, local copies, waits for them, and re-layouts  9.85 us
    dot_general x4, matrix products, body(): lax.dot_general(scaled[:, m * depth:(m + 1) * depth], grads, (((0,), (0,)...  8.57 us
    slice x2, local copies, waits for them, and re-layouts, body(): below_half, above_half = (below[:half], above[half:])  3.64 us
  transfers between devices with their start and end apart: 31, of which 15 were waited for; matrix products, arithmetic and copies ran while one was open for 20% of the time, Pallas kernels for 0%

profile of v2, /device:TPU:1, one launch (start us, length us, event | category | flops | bytes accessed | tf_op | source)
XLA Modules:
  0.0 149.1 jit_solution(1495766849464002091)
XLA Ops:
  2.2 2.2 %collective-permute-start = (bf16[32,1024]{1,0:T(8,128)(2,1)S(1)}, bf16[32,1024]{1,0:T(8,128)(2,1)S(1)}, u32[]{:S(2)}, u32[]{:S(2)}) collective-permute-start(bf16[32,1024]{1,0:T(8,128)(2,1)S(1)} %pad_maximum_fusion.9), channel_id=1, source_target_pairs={{0,64},{64,128},{128,192},{192,0},{1,65},{65,129},{129,193},{193,1... | collective-permute-start | bytes 196616 | tf_op jit(solution)/shard_map/ppermute | solution.py:37
  4.4 2.6 %collective-permute-start.1 = (bf16[32,1024]{1,0:T(8,128)(2,1)S(1)}, bf16[32,1024]{1,0:T(8,128)(2,1)S(1)}, u32[]{:S(2)}, u32[]{:S(2)}) collective-permute-start(bf16[32,1024]{1,0:T(8,128)(2,1)S(1)} %pad_maximum_fusion.10), channel_id=1, source_target_pairs={{0,128},{64,192},{128,0},{192,64},{1,129},{65,193},{129,1},{193,65... | collective-permute-start | bytes 196616 | tf_op jit(solution)/shard_map/ppermute | solution.py:37
  8.1 2.2 %copy.25 = bf16[2,8,32,896]{3,2,1,0:T(8,128)(2,1)} copy(bf16[2,8,32,896]{3,2,0,1:T(8,128)(2,1)} %bitcast.159) | data formatting | bytes 1835008 | tf_op jit(solution)/shard_map/transpose | solution.py:59
  12.5 2.3 %collective-permute-start.6 = (bf16[512,896]{1,0:T(8,128)(2,1)}, bf16[512,896]{1,0:T(8,128)(2,1)}, u32[]{:S(2)}, u32[]{:S(2)}) collective-permute-start(bf16[512,896]{1,0:T(8,128)(2,1)} %bitcast.6), channel_id=1, source_target_pairs={{0,192},{64,0},{128,64},{192,128},{1,193},{65,1},{129,65},{193,129... | collective-permute-start | bytes 2752520 | tf_op jit(solution)/shard_map/ppermute | solution.py:37
  16.9 4.4 %collective-permute-start.4 = (bf16[256,896]{1,0:T(8,128)(2,1)S(1)}, bf16[256,896]{1,0:T(8,128)(2,1)S(1)}, u32[]{:S(2)}, u32[]{:S(2)}) collective-permute-start(bf16[256,896]{1,0:T(8,128)(2,1)S(1)} %fusion.7), channel_id=1, source_target_pairs={{0,48},{16,0},{32,16},{48,32},{1,49},{17,1},{33,17},{49,33},{2,50}... | collective-permute-start | bytes 1376264 | tf_op jit(solution)/shard_map/ppermute | solution.py:37
  21.3 4.2 %collective-permute-start.3 = (bf16[4,32,1024]{2,1,0:T(8,128)(2,1)S(1)}, bf16[4,32,1024]{2,1,0:T(8,128)(2,1)S(1)}, u32[]{:S(2)}, u32[]{:S(2)}) collective-permute-start(bf16[4,32,1024]{2,1,0:T(8,128)(2,1)S(1)} %pad_maximum_fusion.8), channel_id=1, source_target_pairs={{0,2},{2,0},{1,3},{3,1},{4,6},{6,4},{5,7},{7,5},{8,10},{10,8},{9,1... | collective-permute-start | bytes 786440 | tf_op jit(solution)/shard_map/ppermute | solution.py:37
  25.6 8.3 %collective-permute-done.5 = bf16[512,896]{1,0:T(8,128)(2,1)} collective-permute-done((bf16[512,896]{1,0:T(8,128)(2,1)}, bf16[512,896]{1,0:T(8,128)(2,1)}, u32[]{:S(2)}, u32[]{:S(2)}) %collective-permute-start.5) | collective-permute-done | bytes 917536 | tf_op jit(solution)/shard_map/ppermute | solution.py:37
  33.9 1.8 %slice.112 = bf16[256,896]{1,0:T(8,128)(2,1)} slice(bf16[512,896]{1,0:T(8,128)(2,1)} %collective-permute-done.5), slice={[0:256], [0:896]} | slice | bytes 917504 | tf_op jit(solution)/shard_map/slice | solution.py:86
  35.7 1.8 %slice.113 = bf16[256,896]{1,0:T(8,128)(2,1)} slice(bf16[512,896]{1,0:T(8,128)(2,1)} %collective-permute-done.6), slice={[256:512], [0:896]} | slice | bytes 917504 | tf_op jit(solution)/shard_map/slice | solution.py:86
  37.5 7.7 %collective-permute-done.3 = bf16[4,32,1024]{2,1,0:T(8,128)(2,1)S(1)} collective-permute-done((bf16[4,32,1024]{2,1,0:T(8,128)(2,1)S(1)}, bf16[4,32,1024]{2,1,0:T(8,128)(2,1)S(1)}, u32[]{:S(2)}, u32[]{:S(2)}) %collective-permute-start.3) | collective-permute-done | bytes 262176 | tf_op jit(solution)/shard_map/ppermute | solution.py:37
  47.5 1.5 collective-permute-start.11
  49.6 2.7 %collective-permute-start.9 = (bf16[256,896]{1,0:T(8,128)(2,1)}, bf16[256,896]{1,0:T(8,128)(2,1)}, u32[]{:S(2)}, u32[]{:S(2)}) collective-permute-start(bf16[256,896]{1,0:T(8,128)(2,1)} %slice.113), channel_id=1, source_target_pairs={{0,192},{64,0},{128,64},{192,128},{1,193},{65,1},{129,65},{193,129... | collective-permute-start | bytes 1376264 | tf_op jit(solution)/shard_map/ppermute | solution.py:37
  53.6 1.3 constant_dynamic-update-slice_fusion.3
  54.9 2.8 %collective-permute-done.7 = bf16[256,896]{1,0:T(8,128)(2,1)S(1)} collective-permute-done((bf16[256,896]{1,0:T(8,128)(2,1)}, bf16[256,896]{1,0:T(8,128)(2,1)S(1)}, u32[]{:S(2)}, u32[]{:S(2)}) %collective-permute-start.7) | collective-permute-done | bytes 458784 | tf_op jit(solution)/shard_map/ppermute | solution.py:37
  57.6 1.7 %collective-permute-done.8 = bf16[256,896]{1,0:T(8,128)(2,1)} collective-permute-done((bf16[256,896]{1,0:T(8,128)(2,1)}, bf16[256,896]{1,0:T(8,128)(2,1)}, u32[]{:S(2)}, u32[]{:S(2)}) %collective-permute-start.8) | collective-permute-done | bytes 458784 | tf_op jit(solution)/shard_map/ppermute | solution.py:37
  59.3 1.8 %collective-permute-start.16 = (bf16[2,4,32,1024]{3,2,0,1:T(8,128)(2,1)S(1)}, bf16[2,4,32,1024]{3,2,0,1:T(8,128)(2,1)S(1)}, u32[]{:S(2)}, u32[]{:S(2)}) collective-permute-start(bf16[2,4,32,1024]{3,2,0,1:T(8,128)(2,1)S(1)} %broadcast_select_fusion), channel_id=1, source_target_pairs={{0,8},{4,12},{8,0},{12,4},{1,9},{5,13},{9,1},{13,5},{2,10},{6,14},... | collective-permute-start | bytes 1572872 | tf_op jit(solution)/shard_map/ppermute | solution.py:37
  61.3 5.1 %collective-permute-start.17 = (bf16[3,2,4,32,1024]{4,3,1,2,0:T(8,128)(2,1)S(1)}, bf16[3,2,4,32,1024]{4,3,1,2,0:T(8,128)(2,1)S(1)}, u32[]{:S(2)}, u32[]{:S(2)}) collective-permute-start(bf16[3,2,4,32,1024]{4,3,1,2,0:T(8,128)(2,1)S(1)} %pad_maximum_fusion), channel_id=1, source_target_pairs={{0,1},{1,0},{2,3},{3,2},{4,5},{5,4},{6,7},{7,6},{8,9},{9,8},{10,11... | collective-permute-start | bytes 4718600 | tf_op jit(solution)/shard_map/ppermute | solution.py:37
  75.7 1.4 collective-permute-done.18
  80.8 2.3 %collective-permute-start.21 = (bf16[256,896]{1,0:T(8,128)(2,1)S(1)}, bf16[256,896]{1,0:T(8,128)(2,1)S(1)}, u32[]{:S(2)}, u32[]{:S(2)}) collective-permute-start(bf16[256,896]{1,0:T(8,128)(2,1)S(1)} %convolution_convert_fusion.2), channel_id=1, source_target_pairs={{0,48},{16,0},{32,16},{48,32},{1,49},{17,1},{33,17},{49,33},{2,50}... | collective-permute-start | bytes 1376264 | tf_op jit(solution)/shard_map/ppermute | solution.py:37
  87.0 6.0 %collective-permute-done.21 = bf16[256,896]{1,0:T(8,128)(2,1)S(1)} collective-permute-done((bf16[256,896]{1,0:T(8,128)(2,1)S(1)}, bf16[256,896]{1,0:T(8,128)(2,1)S(1)}, u32[]{:S(2)}, u32[]{:S(2)}) %collective-permute-start.21) | collective-permute-done | bytes 458784 | tf_op jit(solution)/shard_map/ppermute | solution.py:37
  93.0 2.1 %add_convert_fusion.1 = bf16[256,896]{1,0:T(8,128)(2,1)} fusion(bf16[256,896]{1,0:T(8,128)(2,1)S(1)} %collective-permute-done.21, bf16[2048,896]{1,0:T(8,128)(2,1)S(1)} %constant_dynamic-update-slice_fusion, bf16[2048,1024]{1,0:T(8,128)(2,1)S(1)} %bitcast.144), kind=kOutput, calls=%fused_computation.23 | convolution fusion | flops 940212224 | bytes 5636096 | tf_op jit(solution)/shard_map/dot_general | solution.py:122
  95.1 4.0 %collective-permute-start.22 = (bf16[256,896]{1,0:T(8,128)(2,1)}, bf16[256,896]{1,0:T(8,128)(2,1)}, u32[]{:S(2)}, u32[]{:S(2)}) collective-permute-start(bf16[256,896]{1,0:T(8,128)(2,1)} %add_convert_fusion.1), channel_id=1, source_target_pairs={{0,48},{16,0},{32,16},{48,32},{1,49},{17,1},{33,17},{49,33},{2,50}... | collective-permute-start | bytes 1376264 | tf_op jit(solution)/shard_map/ppermute | solution.py:37
  106.9 1.4 collective-permute-done.22
  108.3 2.0 %collective-permute-done.23 = bf16[4,64,512]{2,1,0:T(8,128)(2,1)} collective-permute-done((bf16[4,64,512]{2,1,0:T(8,128)(2,1)}, bf16[4,64,512]{2,1,0:T(8,128)(2,1)}, u32[]{:S(2)}, u32[]{:S(2)}) %collective-permute-start.23) | collective-permute-done | bytes 262176 | tf_op jit(solution)/shard_map/ppermute | solution.py:37
  110.3 2.1 %collective-permute-done.24 = bf16[4,64,512]{2,1,0:T(8,128)(2,1)} collective-permute-done((bf16[4,64,512]{2,1,0:T(8,128)(2,1)}, bf16[4,64,512]{2,1,0:T(8,128)(2,1)}, u32[]{:S(2)}, u32[]{:S(2)}) %collective-permute-start.24) | collective-permute-done | bytes 262176 | tf_op jit(solution)/shard_map/ppermute | solution.py:37
  112.5 7.4 %collective-permute-done.25 = bf16[4,64,512]{2,1,0:T(8,128)(2,1)} collective-permute-done((bf16[4,64,512]{2,1,0:T(8,128)(2,1)}, bf16[4,64,512]{2,1,0:T(8,128)(2,1)}, u32[]{:S(2)}, u32[]{:S(2)}) %collective-permute-start.25) | collective-permute-done | bytes 262176 | tf_op jit(solution)/shard_map/ppermute | solution.py:37
  119.9 1.4 fusion.11
  122.3 2.6 %add_convert_fusion = bf16[256,896]{1,0:T(8,128)(2,1)S(1)} fusion(bf16[256,896]{1,0:T(8,128)(2,1)} %collective-permute-done.22, bf16[2048,896]{1,0:T(8,128)(2,1)S(1)} %copy-done.1, bf16[2048,1024]{1,0:T(8,128)(2,1)} %bitcast.145), kind=kOutput, calls=%fused_computation.22 | convolution fusion | flops 940212224 | bytes 5636096 | tf_op jit(solution)/shard_map/dot_general | solution.py:122
  125.1 11.1 %collective-permute-done.26 = bf16[4,32,1024]{2,1,0:T(8,128)(2,1)S(1)} collective-permute-done((bf16[4,32,1024]{2,1,0:T(8,128)(2,1)S(1)}, bf16[4,32,1024]{2,1,0:T(8,128)(2,1)S(1)}, u32[]{:S(2)}, u32[]{:S(2)}) %collective-permute-start.26) | collective-permute-done | bytes 262176 | tf_op jit(solution)/shard_map/ppermute | solution.py:37
  136.5 2.4 %collective-permute-start.27 = (bf16[32,1024]{1,0:T(8,128)(2,1)S(1)}, bf16[32,1024]{1,0:T(8,128)(2,1)S(1)}, u32[]{:S(2)}, u32[]{:S(2)}) collective-permute-start(bf16[32,1024]{1,0:T(8,128)(2,1)S(1)} %get-tuple-element.76), channel_id=1, source_target_pairs={{0,192},{64,0},{128,64},{192,128},{1,193},{65,1},{129,65},{193,129... | collective-permute-start | bytes 196616 | tf_op jit(solution)/shard_map/ppermute | solution.py:37
  140.2 3.3 %collective-permute-done.28 = bf16[32,1024]{1,0:T(8,128)(2,1)S(1)} collective-permute-done((bf16[32,1024]{1,0:T(8,128)(2,1)S(1)}, bf16[32,1024]{1,0:T(8,128)(2,1)S(1)}, u32[]{:S(2)}, u32[]{:S(2)}) %collective-permute-start.28) | collective-permute-done | bytes 65568 | tf_op jit(solution)/shard_map/ppermute | solution.py:37
  143.9 2.6 %convert_multiply_fusion = f32[256,896]{1,0:T(8,128)S(1)} fusion(bf16[256,896]{1,0:T(8,128)(2,1)S(1)} %copy-done.7, bf16[256,896]{1,0:T(8,128)(2,1)S(1)} %collective-permute-done.30, bf16[2048,896]{1,0:T(8,128)(2,1)S(1)} %copy-done.1, bf16[2048,1024]{1,0:T(8,128)(2,1)} %bitcast.146), kind=kOutput, calls=%fused_computation.9 | convolution fusion | flops 940441600 | bytes 6553600 | tf_op jit(solution)/shard_map/dot_general | solution.py:122
  (132 shorter events, 41.1 us)
Async XLA Ops:
  2.2 9.7 %collective-permute-start = (bf16[32,1024]{1,0:T(8,128)(2,1)S(1)}, bf16[32,1024]{1,0:T(8,128)(2,1)S(1)}, u32[]{:S(2)}, u32[]{:S(2)}) collective-permute-start(bf16[32,1024]{1,0:T(8,128)(2,1)S(1)} %pad_maximum_fusion.9), channel_id=1, source_target_pairs={{0,64},{64,128},{128,192},{192,0},{1,65},{65,129},{129,193},{193,1... | collective-permute-start | bytes 196616 | tf_op jit(solution)/shard_map/ppermute | solution.py:37
  4.4 7.5 %collective-permute-start.1 = (bf16[32,1024]{1,0:T(8,128)(2,1)S(1)}, bf16[32,1024]{1,0:T(8,128)(2,1)S(1)}, u32[]{:S(2)}, u32[]{:S(2)}) collective-permute-start(bf16[32,1024]{1,0:T(8,128)(2,1)S(1)} %pad_maximum_fusion.10), channel_id=1, source_target_pairs={{0,128},{64,192},{128,0},{192,64},{1,129},{65,193},{129,1},{193,65... | collective-permute-start | bytes 196616 | tf_op jit(solution)/shard_map/ppermute | solution.py:37
  7.0 4.9 %collective-permute-start.2 = (bf16[32,1024]{1,0:T(8,128)(2,1)S(1)}, bf16[32,1024]{1,0:T(8,128)(2,1)S(1)}, u32[]{:S(2)}, u32[]{:S(2)}) collective-permute-start(bf16[32,1024]{1,0:T(8,128)(2,1)S(1)} %pad_maximum_fusion.11), channel_id=1, source_target_pairs={{0,192},{64,0},{128,64},{192,128},{1,193},{65,1},{129,65},{193,129... | collective-permute-start | bytes 196616 | tf_op jit(solution)/shard_map/ppermute | solution.py:37
  12.0 21.9 %collective-permute-start.5 = (bf16[512,896]{1,0:T(8,128)(2,1)}, bf16[512,896]{1,0:T(8,128)(2,1)}, u32[]{:S(2)}, u32[]{:S(2)}) collective-permute-start(bf16[512,896]{1,0:T(8,128)(2,1)} %bitcast.6), channel_id=1, source_target_pairs={{0,64},{64,128},{128,192},{192,0},{1,65},{65,129},{129,193},{193,1... | collective-permute-start | bytes 2752520 | tf_op jit(solution)/shard_map/ppermute | solution.py:37
  12.5 23.3 %collective-permute-start.6 = (bf16[512,896]{1,0:T(8,128)(2,1)}, bf16[512,896]{1,0:T(8,128)(2,1)}, u32[]{:S(2)}, u32[]{:S(2)}) collective-permute-start(bf16[512,896]{1,0:T(8,128)(2,1)} %bitcast.6), channel_id=1, source_target_pairs={{0,192},{64,0},{128,64},{192,128},{1,193},{65,1},{129,65},{193,129... | collective-permute-start | bytes 2752520 | tf_op jit(solution)/shard_map/ppermute | solution.py:37
  16.9 28.4 %copy-start.8 = (bf16[256,896]{1,0:T(8,128)(2,1)}, bf16[256,896]{1,0:T(8,128)(2,1)S(1)}, u32[]{:S(2)}) copy-start(bf16[256,896]{1,0:T(8,128)(2,1)S(1)} %fusion.7) | copy-start | bytes 1376260
  16.9 28.4 %collective-permute-start.4 = (bf16[256,896]{1,0:T(8,128)(2,1)S(1)}, bf16[256,896]{1,0:T(8,128)(2,1)S(1)}, u32[]{:S(2)}, u32[]{:S(2)}) collective-permute-start(bf16[256,896]{1,0:T(8,128)(2,1)S(1)} %fusion.7), channel_id=1, source_target_pairs={{0,48},{16,0},{32,16},{48,32},{1,49},{17,1},{33,17},{49,33},{2,50}... | collective-permute-start | bytes 1376264 | tf_op jit(solution)/shard_map/ppermute | solution.py:37
  21.3 23.9 %collective-permute-start.3 = (bf16[4,32,1024]{2,1,0:T(8,128)(2,1)S(1)}, bf16[4,32,1024]{2,1,0:T(8,128)(2,1)S(1)}, u32[]{:S(2)}, u32[]{:S(2)}) collective-permute-start(bf16[4,32,1024]{2,1,0:T(8,128)(2,1)S(1)} %pad_maximum_fusion.8), channel_id=1, source_target_pairs={{0,2},{2,0},{1,3},{3,1},{4,6},{6,4},{5,7},{7,5},{8,10},{10,8},{9,1... | collective-permute-start | bytes 786440 | tf_op jit(solution)/shard_map/ppermute | solution.py:37
  46.2 13.2 %collective-permute-start.10 = (bf16[2,4,32,1024]{3,2,0,1:T(8,128)(2,1)S(1)}, bf16[2,4,32,1024]{3,2,0,1:T(8,128)(2,1)S(1)}, u32[]{:S(2)}, u32[]{:S(2)}) collective-permute-start(bf16[2,4,32,1024]{3,2,0,1:T(8,128)(2,1)S(1)} %broadcast_select_fusion), channel_id=1, source_target_pairs={{0,4},{4,8},{8,12},{12,0},{1,5},{5,9},{9,13},{13,1},{2,6},{6,10},{... | collective-permute-start | bytes 1572872 | tf_op jit(solution)/shard_map/ppermute | solution.py:37
  47.5 11.9 %collective-permute-start.11 = (bf16[2,4,32,1024]{3,2,0,1:T(8,128)(2,1)S(1)}, bf16[2,4,32,1024]{3,2,0,1:T(8,128)(2,1)S(1)}, u32[]{:S(2)}, u32[]{:S(2)}) collective-permute-start(bf16[2,4,32,1024]{3,2,0,1:T(8,128)(2,1)S(1)} %broadcast_select_fusion), channel_id=1, source_target_pairs={{0,12},{4,0},{8,4},{12,8},{1,13},{5,1},{9,5},{13,9},{2,14},{6,2},{... | collective-permute-start | bytes 1572872 | tf_op jit(solution)/shard_map/ppermute | solution.py:37
  48.9 8.7 %collective-permute-start.7 = (bf16[256,896]{1,0:T(8,128)(2,1)}, bf16[256,896]{1,0:T(8,128)(2,1)S(1)}, u32[]{:S(2)}, u32[]{:S(2)}) collective-permute-start(bf16[256,896]{1,0:T(8,128)(2,1)} %copy-done.14), channel_id=1, source_target_pairs={{0,48},{16,0},{32,16},{48,32},{1,49},{17,1},{33,17},{49,33},{2,50}... | collective-permute-start | bytes 1376264 | tf_op jit(solution)/shard_map/ppermute | solution.py:37
  49.6 9.7 %collective-permute-start.8 = (bf16[256,896]{1,0:T(8,128)(2,1)}, bf16[256,896]{1,0:T(8,128)(2,1)}, u32[]{:S(2)}, u32[]{:S(2)}) collective-permute-start(bf16[256,896]{1,0:T(8,128)(2,1)} %slice.112), channel_id=1, source_target_pairs={{0,64},{64,128},{128,192},{192,0},{1,65},{65,129},{129,193},{193,1... | collective-permute-start | bytes 1376264 | tf_op jit(solution)/shard_map/ppermute | solution.py:37
  49.6 9.7 %collective-permute-start.9 = (bf16[256,896]{1,0:T(8,128)(2,1)}, bf16[256,896]{1,0:T(8,128)(2,1)}, u32[]{:S(2)}, u32[]{:S(2)}) collective-permute-start(bf16[256,896]{1,0:T(8,128)(2,1)} %slice.113), channel_id=1, source_target_pairs={{0,192},{64,0},{128,64},{192,128},{1,193},{65,1},{129,65},{193,129... | collective-permute-start | bytes 1376264 | tf_op jit(solution)/shard_map/ppermute | solution.py:37
  59.3 15.4 %collective-permute-start.16 = (bf16[2,4,32,1024]{3,2,0,1:T(8,128)(2,1)S(1)}, bf16[2,4,32,1024]{3,2,0,1:T(8,128)(2,1)S(1)}, u32[]{:S(2)}, u32[]{:S(2)}) collective-permute-start(bf16[2,4,32,1024]{3,2,0,1:T(8,128)(2,1)S(1)} %broadcast_select_fusion), channel_id=1, source_target_pairs={{0,8},{4,12},{8,0},{12,4},{1,9},{5,13},{9,1},{13,5},{2,10},{6,14},... | collective-permute-start | bytes 1572872 | tf_op jit(solution)/shard_map/ppermute | solution.py:37
  61.3 13.4 %collective-permute-start.17 = (bf16[3,2,4,32,1024]{4,3,1,2,0:T(8,128)(2,1)S(1)}, bf16[3,2,4,32,1024]{4,3,1,2,0:T(8,128)(2,1)S(1)}, u32[]{:S(2)}, u32[]{:S(2)}) collective-permute-start(bf16[3,2,4,32,1024]{4,3,1,2,0:T(8,128)(2,1)S(1)} %pad_maximum_fusion), channel_id=1, source_target_pairs={{0,1},{1,0},{2,3},{3,2},{4,5},{5,4},{6,7},{7,6},{8,9},{9,8},{10,11... | collective-permute-start | bytes 4718600 | tf_op jit(solution)/shard_map/ppermute | solution.py:37
  66.5 12.1 %collective-permute-start.19 = (bf16[256,896]{1,0:T(8,128)(2,1)S(1)}, bf16[256,896]{1,0:T(8,128)(2,1)S(1)}, u32[]{:S(2)}, u32[]{:S(2)}) collective-permute-start(bf16[256,896]{1,0:T(8,128)(2,1)S(1)} %collective-permute-done.7), channel_id=1, source_target_pairs={{0,48},{16,0},{32,16},{48,32},{1,49},{17,1},{33,17},{49,33},{2,50}... | collective-permute-start | bytes 1376264 | tf_op jit(solution)/shard_map/ppermute | solution.py:37
  73.6 9.6 %collective-permute-start.12 = (bf16[1024,512]{1,0:T(8,128)(2,1)S(1)}, bf16[1024,512]{1,0:T(8,128)(2,1)S(1)}, u32[]{:S(2)}, u32[]{:S(2)}) collective-permute-start(bf16[1024,512]{1,0:T(8,128)(2,1)S(1)} %convolution_convert_fusion.1), channel_id=1, source_target_pairs={{0,1},{1,0},{2,3},{3,2},{4,5},{5,4},{6,7},{7,6},{8,9},{9,8},{10,11... | collective-permute-start | bytes 3145736 | tf_op jit(solution)/shard_map/ppermute | solution.py:37
  74.8 2.3 %collective-permute-start.18 = (bf16[2,4,32,1024]{3,2,0,1:T(8,128)(2,1)S(1)}, bf16[2,4,32,1024]{3,2,0,1:T(8,128)(2,1)S(1)}, u32[]{:S(2)}, u32[]{:S(2)}) collective-permute-start(bf16[2,4,32,1024]{3,2,0,1:T(8,128)(2,1)S(1)} %collective-permute-done.16), channel_id=1, source_target_pairs={{0,1},{1,0},{2,3},{3,2},{4,5},{5,4},{6,7},{7,6},{8,9},{9,8},{10,11... | collective-permute-start | bytes 1572872 | tf_op jit(solution)/shard_map/ppermute | solution.py:37
  79.9 19.2 %collective-permute-start.20 = (bf16[1024,512]{1,0:T(8,128)(2,1)S(1)}, bf16[1024,512]{1,0:T(8,128)(2,1)S(1)}, u32[]{:S(2)}, u32[]{:S(2)}) collective-permute-start(bf16[1024,512]{1,0:T(8,128)(2,1)S(1)} %convolution_convert_fusion), channel_id=1, source_target_pairs={{0,1},{1,0},{2,3},{3,2},{4,5},{5,4},{6,7},{7,6},{8,9},{9,8},{10,11... | collective-permute-start | bytes 3145736 | tf_op jit(solution)/shard_map/ppermute | solution.py:37
  80.8 12.2 %collective-permute-start.21 = (bf16[256,896]{1,0:T(8,128)(2,1)S(1)}, bf16[256,896]{1,0:T(8,128)(2,1)S(1)}, u32[]{:S(2)}, u32[]{:S(2)}) collective-permute-start(bf16[256,896]{1,0:T(8,128)(2,1)S(1)} %convolution_convert_fusion.2), channel_id=1, source_target_pairs={{0,48},{16,0},{32,16},{48,32},{1,49},{17,1},{33,17},{49,33},{2,50}... | collective-permute-start | bytes 1376264 | tf_op jit(solution)/shard_map/ppermute | solution.py:37
  84.6 17.3 %collective-permute-start.13 = (bf16[4,64,512]{2,1,0:T(8,128)(2,1)S(1)}, bf16[4,64,512]{2,1,0:T(8,128)(2,1)S(1)}, u32[]{:S(2)}, u32[]{:S(2)}) collective-permute-start(bf16[4,64,512]{2,1,0:T(8,128)(2,1)S(1)} %get-tuple-element.69), channel_id=1, source_target_pairs={{0,12},{4,0},{8,4},{12,8},{1,13},{5,1},{9,5},{13,9},{2,14},{6,2},{... | collective-permute-start | bytes 786440 | tf_op jit(solution)/shard_map/ppermute | solution.py:37
  85.6 16.4 %collective-permute-start.14 = (bf16[4,64,512]{2,1,0:T(8,128)(2,1)S(1)}, bf16[4,64,512]{2,1,0:T(8,128)(2,1)S(1)}, u32[]{:S(2)}, u32[]{:S(2)}) collective-permute-start(bf16[4,64,512]{2,1,0:T(8,128)(2,1)S(1)} %get-tuple-element.68), channel_id=1, source_target_pairs={{0,8},{4,12},{8,0},{12,4},{1,9},{5,13},{9,1},{13,5},{2,10},{6,14},... | collective-permute-start | bytes 786440 | tf_op jit(solution)/shard_map/ppermute | solution.py:37
  86.8 15.1 %collective-permute-start.15 = (bf16[4,64,512]{2,1,0:T(8,128)(2,1)S(1)}, bf16[4,64,512]{2,1,0:T(8,128)(2,1)S(1)}, u32[]{:S(2)}, u32[]{:S(2)}) collective-permute-start(bf16[4,64,512]{2,1,0:T(8,128)(2,1)S(1)} %get-tuple-element.67), channel_id=1, source_target_pairs={{0,4},{4,8},{8,12},{12,0},{1,5},{5,9},{9,13},{13,1},{2,6},{6,10},{... | collective-permute-start | bytes 786440 | tf_op jit(solution)/shard_map/ppermute | solution.py:37
  95.1 13.3 %collective-permute-start.22 = (bf16[256,896]{1,0:T(8,128)(2,1)}, bf16[256,896]{1,0:T(8,128)(2,1)}, u32[]{:S(2)}, u32[]{:S(2)}) collective-permute-start(bf16[256,896]{1,0:T(8,128)(2,1)} %add_convert_fusion.1), channel_id=1, source_target_pairs={{0,48},{16,0},{32,16},{48,32},{1,49},{17,1},{33,17},{49,33},{2,50}... | collective-permute-start | bytes 1376264 | tf_op jit(solution)/shard_map/ppermute | solution.py:37
  103.4 7.0 %collective-permute-start.23 = (bf16[4,64,512]{2,1,0:T(8,128)(2,1)}, bf16[4,64,512]{2,1,0:T(8,128)(2,1)}, u32[]{:S(2)}, u32[]{:S(2)}) collective-permute-start(bf16[4,64,512]{2,1,0:T(8,128)(2,1)} %get-tuple-element.51), channel_id=1, source_target_pairs={{0,12},{4,0},{8,4},{12,8},{1,13},{5,1},{9,5},{13,9},{2,14},{6,2},{... | collective-permute-start | bytes 786440 | tf_op jit(solution)/shard_map/ppermute | solution.py:37
  104.2 8.2 %collective-permute-start.24 = (bf16[4,64,512]{2,1,0:T(8,128)(2,1)}, bf16[4,64,512]{2,1,0:T(8,128)(2,1)}, u32[]{:S(2)}, u32[]{:S(2)}) collective-permute-start(bf16[4,64,512]{2,1,0:T(8,128)(2,1)} %get-tuple-element.52), channel_id=1, source_target_pairs={{0,8},{4,12},{8,0},{12,4},{1,9},{5,13},{9,1},{13,5},{2,10},{6,14},... | collective-permute-start | bytes 786440 | tf_op jit(solution)/shard_map/ppermute | solution.py:37
  105.4 14.4 %collective-permute-start.25 = (bf16[4,64,512]{2,1,0:T(8,128)(2,1)}, bf16[4,64,512]{2,1,0:T(8,128)(2,1)}, u32[]{:S(2)}, u32[]{:S(2)}) collective-permute-start(bf16[4,64,512]{2,1,0:T(8,128)(2,1)} %get-tuple-element.53), channel_id=1, source_target_pairs={{0,4},{4,8},{8,12},{12,0},{1,5},{5,9},{9,13},{13,1},{2,6},{6,10},{... | collective-permute-start | bytes 786440 | tf_op jit(solution)/shard_map/ppermute | solution.py:37
  121.4 14.8 %collective-permute-start.26 = (bf16[4,32,1024]{2,1,0:T(8,128)(2,1)S(1)}, bf16[4,32,1024]{2,1,0:T(8,128)(2,1)S(1)}, u32[]{:S(2)}, u32[]{:S(2)}) collective-permute-start(bf16[4,32,1024]{2,1,0:T(8,128)(2,1)S(1)} %fusion.15), channel_id=1, source_target_pairs={{0,2},{2,0},{1,3},{3,1},{4,6},{6,4},{5,7},{7,5},{8,10},{10,8},{9,1... | collective-permute-start | bytes 786440 | tf_op jit(solution)/shard_map/ppermute | solution.py:37
  125.0 18.9 %collective-permute-start.30 = (bf16[256,896]{1,0:T(8,128)(2,1)S(1)}, bf16[256,896]{1,0:T(8,128)(2,1)S(1)}, u32[]{:S(2)}, u32[]{:S(2)}) collective-permute-start(bf16[256,896]{1,0:T(8,128)(2,1)S(1)} %add_convert_fusion), channel_id=1, source_target_pairs={{0,48},{16,0},{32,16},{48,32},{1,49},{17,1},{33,17},{49,33},{2,50}... | collective-permute-start | bytes 1376264 | tf_op jit(solution)/shard_map/ppermute | solution.py:37
  136.5 3.7 %collective-permute-start.27 = (bf16[32,1024]{1,0:T(8,128)(2,1)S(1)}, bf16[32,1024]{1,0:T(8,128)(2,1)S(1)}, u32[]{:S(2)}, u32[]{:S(2)}) collective-permute-start(bf16[32,1024]{1,0:T(8,128)(2,1)S(1)} %get-tuple-element.76), channel_id=1, source_target_pairs={{0,192},{64,0},{128,64},{192,128},{1,193},{65,1},{129,65},{193,129... | collective-permute-start | bytes 196616 | tf_op jit(solution)/shard_map/ppermute | solution.py:37
  138.8 4.7 %collective-permute-start.28 = (bf16[32,1024]{1,0:T(8,128)(2,1)S(1)}, bf16[32,1024]{1,0:T(8,128)(2,1)S(1)}, u32[]{:S(2)}, u32[]{:S(2)}) collective-permute-start(bf16[32,1024]{1,0:T(8,128)(2,1)S(1)} %get-tuple-element.75), channel_id=1, source_target_pairs={{0,128},{64,192},{128,0},{192,64},{1,129},{65,193},{129,1},{193,65... | collective-permute-start | bytes 196616 | tf_op jit(solution)/shard_map/ppermute | solution.py:37
  138.8 5.0 %collective-permute-start.29 = (bf16[32,1024]{1,0:T(8,128)(2,1)S(1)}, bf16[32,1024]{1,0:T(8,128)(2,1)S(1)}, u32[]{:S(2)}, u32[]{:S(2)}) collective-permute-start(bf16[32,1024]{1,0:T(8,128)(2,1)S(1)} %get-tuple-element.74), channel_id=1, source_target_pairs={{0,64},{64,128},{128,192},{192,0},{1,65},{65,129},{129,193},{193,1... | collective-permute-start | bytes 196616 | tf_op jit(solution)/shard_map/ppermute | solution.py:37
  (15 other events, 103.7 us)
